TPU v7x, 32 devices: a whole 2x2x4 slice. The times are simulated.
32 devices in a mesh: dp: 8 (over z, x), tensor: 4 (over y, core).
Axes of the slice: x: 2, y: 2, z: 4, core: 2. Of those that a mesh axis runs over, the one named last changes fastest.
Arguments:
- rollout_states: bfloat16 [8192, 8192], P('dp', 'tensor'), may hold values from -6 to 6
- norm_gain: float32 [8192], replicated, may hold values from 0.1 to 1.9
- w_query: bfloat16 [8192, 4096], P('dp', 'tensor'), as said below
- w_key: bfloat16 [8192, 512], P('dp', 'tensor'), as said below
- w_value: bfloat16 [8192, 512], P('dp', 'tensor'), may hold values from -0.0625 to 0.0625
- b_query: float32 [4096], P('tensor'), may hold values from -3 to 3
- b_key: float32 [512], P('tensor'), may hold values from -3 to 3
- b_value: float32 [512], P('tensor'), may hold values from -3 to 3
- seq_lengths: int32 [64], replicated, may hold values from 1 to 255, as said below
- seq_dest: int32 [64], replicated, may hold values from 0 to 7, as said below
- seq_offset: int32 [64], replicated, may hold values from 0 to 1023, as said below
Outputs:
- context: bfloat16 [8192, 4096], P('dp', 'tensor')
Inputs may be any that keep to these rules, and one draw needn't show every extreme that they name: `seq_lengths`: the 8 responses r * 8 to r * 8 + 7 lie in this order in rollout device r's 1024 rows and fill them; some response has exactly 255 tokens. `seq_dest`: the responses of one rollout device go to 8 different learners, so every learner receives exactly one response from every rollout device. `seq_offset`: the responses of one learner occupy disjoint runs of rows that together cover its 1024 rows. `w_query`: A weight matrix. `w_key`: A weight matrix.
All inputs are finite; a program needn't handle non-finite values.
Results may differ from a plain program's by a relative error of at most 0.012.
The roundings to bfloat16 on the way count: a program that leaves them out, or rounds other values in their place, can miss the bound.
Values may be sent and summed in bfloat16 or wider, within the bound.
No kernel may reach another device: no remote copies, remote signals or barrier semaphores. Data moves between devices by JAX's collectives and lax.ppermute only.
A program may use at most 128 MiB of HBM per device.

v0:
```python
import functools

import jax
import jax.numpy as jnp
from jax import lax
from jax.experimental import pallas as pl
from jax.experimental.pallas import tpu as pltpu
from jax.sharding import PartitionSpec as P

HD = 128

rope_base = 1000000.0
norm_eps = 1e-06
mask_value = -1e30
kernel_cost = pl.CostEstimate(flops=4 * 10**9, bytes_accessed=2**20, transcendentals=0)


def rope_tables(positions):
    half_dim = HD // 2
    frequency = rope_base ** (-(jnp.arange(half_dim).astype(jnp.float32) * 2.0 / HD))
    angles = positions.astype(jnp.float32)[:, None] * frequency[None, :]
    return (jnp.cos(angles), jnp.sin(angles))


def rotate(states, cosine, sine):
    half_dim = states.shape[-1] // 2
    first_half = states[..., :half_dim]
    second_half = states[..., half_dim:]
    cos_wide = cosine[:, None, :]
    sin_wide = sine[:, None, :]
    return jnp.concatenate(
        [
            first_half * cos_wide - second_half * sin_wide,
            second_half * cos_wide + first_half * sin_wide,
        ],
        axis=-1,
    )


def local_any(
    rollout_states,
    norm_gain,
    w_query,
    w_key,
    w_value,
    b_query,
    b_key,
    b_value,
    seq_lengths,
    seq_dest,
    seq_offset,
):
    learners = lax.axis_size("dp")
    own_index = lax.axis_index("dp")
    row_count, feature_count = rollout_states.shape
    capacity = 2 * row_count // learners - 1
    lengths = seq_lengths.reshape(learners, learners)
    dests = seq_dest.reshape(learners, learners)
    offsets = seq_offset.reshape(learners, learners)
    starts = jnp.cumsum(lengths, axis=1) - lengths
    peer_ids = jnp.arange(learners, dtype=jnp.int32)
    own_length = lax.dynamic_index_in_dim(lengths, own_index, 0, keepdims=False)
    own_start = lax.dynamic_index_in_dim(starts, own_index, 0, keepdims=False)
    own_dest = lax.dynamic_index_in_dim(dests, own_index, 0, keepdims=False)
    match_send = (own_dest[None, :] == peer_ids[:, None]).astype(jnp.int32)
    send_start = jnp.sum(match_send * own_start[None, :], axis=1)
    send_length = jnp.sum(match_send * own_length[None, :], axis=1)
    slot_index = jnp.arange(capacity, dtype=jnp.int32)
    pick_rows = send_start[:, None] + slot_index[None, :]
    padded = jnp.concatenate(
        [rollout_states, jnp.zeros((capacity, feature_count), rollout_states.dtype)], axis=0
    )
    live_slots = (slot_index[None, :] < send_length[:, None])[..., None]
    outgoing = jnp.where(
        live_slots, jnp.take(padded, pick_rows, axis=0), jnp.zeros((), rollout_states.dtype)
    )
    incoming = lax.all_to_all(outgoing, "dp", split_axis=0, concat_axis=0, tiled=True)
    matched = (dests == own_index).astype(jnp.int32)
    run_start = jnp.sum(matched * offsets, axis=1)
    run_length = jnp.sum(matched * lengths, axis=1)
    rows = jnp.arange(row_count, dtype=jnp.int32)
    inside = (
        (rows[:, None] >= run_start[None, :]) & (rows[:, None] < (run_start + run_length)[None, :])
    ).astype(jnp.int32)
    source_ids = jnp.sum(inside * peer_ids[None, :], axis=1)
    within_seq = rows - jnp.sum(inside * run_start[None, :], axis=1)
    arrived = jnp.take(
        incoming.reshape(learners * capacity, feature_count),
        source_ids * capacity + within_seq,
        axis=0,
    )
    gathered = lax.all_gather(arrived, "tensor", axis=1, tiled=True)
    widened = gathered.astype(jnp.float32)
    statistic = jnp.mean(widened * widened, axis=-1, keepdims=True)
    normed = (widened * lax.rsqrt(statistic + norm_eps) * norm_gain[None, :]).astype(jnp.bfloat16)
    full_query, full_key, full_value = (
        lax.all_gather(w_query, "dp", axis=0, tiled=True),
        lax.all_gather(w_key, "dp", axis=0, tiled=True),
        lax.all_gather(w_value, "dp", axis=0, tiled=True),
    )
    query = jnp.dot(normed, full_query, preferred_element_type=jnp.float32)
    key = jnp.dot(normed, full_key, preferred_element_type=jnp.float32)
    value = jnp.dot(normed, full_value, preferred_element_type=jnp.float32)
    query = query + b_query[None, :]
    key = key + b_key[None, :]
    value = value + b_value[None, :]
    heads_here = query.shape[1] // HD
    kv_here = key.shape[1] // HD
    group = heads_here // kv_here
    cosine, sine = rope_tables(within_seq)
    rot_query = rotate(query.reshape(row_count, heads_here, HD), cosine, sine).astype(jnp.bfloat16)
    rot_query = rot_query.reshape(row_count, kv_here, group, HD)
    rot_key = rotate(key.reshape(row_count, kv_here, HD), cosine, sine).astype(jnp.bfloat16)
    value_bf = value.reshape(row_count, kv_here, HD).astype(jnp.bfloat16)
    block_rows = min(512, row_count)

    def one_block(block_number):
        first_row = block_number * block_rows
        query_block = lax.dynamic_slice_in_dim(rot_query, first_row, block_rows, 0)
        query_source = lax.dynamic_slice_in_dim(source_ids, first_row, block_rows, 0)
        query_rows = first_row + jnp.arange(block_rows, dtype=jnp.int32)
        scores = jnp.einsum(
            "bcgd,kcd->cgbk", query_block, rot_key, preferred_element_type=jnp.float32
        )
        scores = scores * HD ** (-0.5)
        allowed = (source_ids[None, :] == query_source[:, None]) & (
            rows[None, :] <= query_rows[:, None]
        )
        scores = jnp.where(allowed[None, None], scores, mask_value)
        peak = jnp.max(scores, axis=-1, keepdims=True)
        raised = jnp.exp(scores - peak)
        weights = (raised / jnp.sum(raised, axis=-1, keepdims=True)).astype(jnp.bfloat16)
        context = jnp.einsum(
            "cgbk,kcd->bcgd", weights, value_bf, preferred_element_type=jnp.float32
        )
        return context.astype(jnp.bfloat16).reshape(block_rows, heads_here * HD)

    outputs = lax.map(one_block, jnp.arange(row_count // block_rows, dtype=jnp.int32))
    return outputs.reshape(row_count, heads_here * HD)


def pack_kernel(counts, *refs):
    refs = list(refs)
    pieces = [[refs.pop(0) for _ in range(n)] for n in counts]
    out_ref, sems = refs
    copies = []
    for i, block in enumerate(pieces):
        first = 0
        for n, piece in enumerate(block):
            rows = piece.shape[0]
            copies.append(
                pltpu.make_async_copy(piece, out_ref.at[i, pl.ds(first, rows)], sems.at[i, n])
            )
            first += rows
    for copy in copies:
        copy.start()
    for copy in copies:
        copy.wait()


def pack(blocks, in_vmem):
    counts = tuple(len(pieces) for pieces in blocks)
    rows = sum(piece.shape[0] for piece in blocks[0])
    feats = blocks[0][0].shape[1]
    operands = [piece for pieces in blocks for piece in pieces]
    shape = (len(blocks), rows, feats)
    if in_vmem:
        space, out_shape = pltpu.VMEM, pltpu.VMEM(shape, jnp.bfloat16)
    else:
        space, out_shape = pl.ANY, jax.ShapeDtypeStruct(shape, jnp.bfloat16)
    return pl.pallas_call(
        functools.partial(pack_kernel, counts),
        in_specs=[pl.BlockSpec(memory_space=pl.ANY)] * len(operands),
        out_specs=pl.BlockSpec(memory_space=space),
        out_shape=out_shape,
        scratch_shapes=[pltpu.SemaphoreType.DMA((len(blocks), 2))],
        compiler_params=pltpu.CompilerParams(vmem_limit_bytes=4 * 2**20),
        cost_estimate=kernel_cost,
    )(*operands)


def product_kernel(x_count, ropes, chunks, out_lanes, which_ref, *refs):
    refs = list(refs)
    x_refs = [refs.pop(0) for _ in range(x_count)]
    w_ref = refs.pop(0)
    if ropes:
        part_ref, bias_ref, angle_ref = (refs.pop(0) for _ in range(3))
    out_refs = [refs.pop(0) for _ in out_lanes]
    w_buf, sems = refs
    rows = out_refs[0].shape[0]
    part_rows = x_refs[0].shape[1]
    tile = min(512, part_rows)
    wide = w_ref.shape[3]
    copies = [
        [
            pltpu.make_async_copy(
                w_ref.at[which_ref[i], chunk],
                w_buf.at[i, :, pl.ds(n * wide, wide)],
                sems.at[i, n],
            )
            for n, chunk in enumerate(chunks)
        ]
        for i in range(4)
    ]
    for block in copies:
        for copy in block:
            copy.start()

    for first, x_ref in zip(range(0, rows, part_rows), x_refs):
        if first == 0:
            for block in copies:
                for copy in block:
                    copy.wait()

        @pl.loop(0, part_rows, step=tile)
        def _(at, first=first, x_ref=x_ref):
            here = pl.ds(pl.multiple_of(first + at, tile), tile)
            term = None
            for i in range(4):
                rows_here = x_ref[i, pl.ds(pl.multiple_of(at, tile), tile), :]
                dot = jnp.dot(rows_here, w_buf[i], preferred_element_type=jnp.float32)
                term = dot if term is None else term + dot
            if not ropes:
                for out_ref, (low, high) in zip(out_refs, out_lanes):
                    out_ref[here, :] = term[:, low:high].astype(out_ref.dtype)
                return
            (out_ref,) = out_refs
            term = term + part_ref[here, :].astype(jnp.float32) + bias_ref[...]
            angle = angle_ref[here, :]
            turned_angle = pltpu.roll(angle, HD // 2, 1)
            low = lax.broadcasted_iota(jnp.int32, angle.shape, 1) < HD // 2
            cosine = jnp.where(low, angle, turned_angle)
            sine = jnp.where(low, -turned_angle, angle)
            for c, rope in enumerate(ropes):
                head = term[:, c * HD : (c + 1) * HD]
                if rope:
                    head = head * cosine + pltpu.roll(head, HD // 2, 1) * sine
                out_ref[here, c * HD : (c + 1) * HD] = head.astype(out_ref.dtype)


def keep(array):
    return pltpu.with_memory_space_constraint(array, pltpu.VMEM)


def projection(which, x_parts, weights, chunks, outs, finish=None):
    rows = sum(part.shape[1] for part in x_parts)
    feats, columns = weights.shape[2], weights.shape[3] * len(chunks)
    vmem = pl.BlockSpec(memory_space=pltpu.VMEM)
    operands = list(x_parts)
    in_specs = [vmem] * len(operands) + [pl.BlockSpec(memory_space=pl.ANY)]
    operands.append(weights)
    ropes = None
    if finish is not None:
        ropes, part, bias, angles = finish
        operands += [keep(part), bias, angles]
        in_specs += [vmem] * 3
    return pl.pallas_call(
        functools.partial(
            product_kernel,
            len(x_parts),
            ropes,
            tuple(chunks),
            tuple((first, last) for first, last, _ in outs),
        ),
        in_specs=[pl.BlockSpec(memory_space=pltpu.SMEM)] + in_specs,
        out_specs=[vmem] * len(outs),
        out_shape=[pltpu.VMEM((rows, last - first), kind) for first, last, kind in outs],
        scratch_shapes=[
            pltpu.VMEM((4, feats, columns), jnp.bfloat16),
            pltpu.SemaphoreType.DMA((4, len(chunks))),
        ],
        compiler_params=pltpu.CompilerParams(vmem_limit_bytes=(10 + columns // 128) * 2**20),
        cost_estimate=kernel_cost,
    )(which, *operands)


def pick_rows(start, length, slot, window, ref, lanes=slice(None)):
    first = pl.multiple_of(jnp.minimum((start // 16) * 16, ref.shape[0] - window), 16)
    row_at = lax.broadcasted_iota(jnp.int32, (slot, window), 0)
    col_at = lax.broadcasted_iota(jnp.int32, (slot, window), 1)
    pick = jnp.where((col_at == row_at + (start - first)) & (row_at < length), 1.0, 0.0)
    rows = jnp.dot(
        pick.astype(jnp.bfloat16), ref[pl.ds(first, window), lanes], preferred_element_type=jnp.float32
    )
    return rows.astype(jnp.bfloat16)


def slots_kernel(slot, window, start_ref, len_ref, in_ref, out_ref):
    for s in range(out_ref.shape[0]):
        out_ref[s] = pick_rows(start_ref[s], len_ref[s], slot, window, in_ref)


def to_slots(starts, lens, array, slot, window):
    count, columns = starts.shape[0], array.shape[1]
    scalars = pl.BlockSpec(memory_space=pltpu.SMEM)
    vmem = pl.BlockSpec(memory_space=pltpu.VMEM)
    return pl.pallas_call(
        functools.partial(slots_kernel, slot, window),
        in_specs=[scalars, scalars, vmem],
        out_specs=vmem,
        out_shape=pltpu.VMEM((count, slot, columns), jnp.bfloat16),
        compiler_params=pltpu.CompilerParams(vmem_limit_bytes=5 * 2**20),
        cost_estimate=kernel_cost,
    )(starts, lens, keep(array))


def attend_kernel(heads, window, start_ref, len_ref, q_ref, kv_ref, *out_refs):
    if len(out_refs) == 1:
        (whole_ref,) = out_refs
        out_refs = [whole_ref.at[s] for s in range(whole_ref.shape[0])]
    slot = out_refs[0].shape[0]
    half = slot // 2
    for s, out_ref in enumerate(out_refs):
        query = pick_rows(start_ref[s], len_ref[s], slot, window, q_ref)
        for block in range(2):
            width = (block + 1) * half
            stacked = jnp.concatenate(
                [query[block * half : width, h * HD : (h + 1) * HD] for h in range(heads)], axis=0
            )
            scores = lax.dot_general(
                stacked,
                kv_ref[s, :width, :HD],
                (((1,), (1,)), ((), ())),
                preferred_element_type=jnp.float32,
            )
            row_at = lax.broadcasted_iota(jnp.int32, scores.shape, 0) & (half - 1)
            col_at = lax.broadcasted_iota(jnp.int32, scores.shape, 1)
            scores = jnp.where(col_at <= row_at + block * half, scores * HD ** (-0.5), mask_value)
            peak = jnp.max(scores, axis=-1, keepdims=True)
            raised = jnp.exp(scores - peak)
            weights = raised * (1.0 / jnp.sum(raised, axis=-1, keepdims=True))
            context = jnp.dot(
                weights.astype(jnp.bfloat16),
                kv_ref[s, :width, HD:],
                preferred_element_type=jnp.float32,
            ).astype(out_ref.dtype)
            for h in range(heads):
                out_ref[block * half : width, h * HD : (h + 1) * HD] = context[
                    h * half : (h + 1) * half
                ]


def attend(starts, lens, query, kv_slots, window, apart):
    columns = query.shape[1]
    count, slot = kv_slots.shape[:2]
    scalars = pl.BlockSpec(memory_space=pltpu.SMEM)
    vmem = pl.BlockSpec(memory_space=pltpu.VMEM)
    return pl.pallas_call(
        functools.partial(attend_kernel, columns // HD, window),
        in_specs=[scalars, scalars, vmem, vmem],
        out_specs=[vmem] * count if apart else vmem,
        out_shape=(
            [pltpu.VMEM((slot, columns), jnp.bfloat16)] * count
            if apart
            else pltpu.VMEM((count, slot, columns), jnp.bfloat16)
        ),
        compiler_params=pltpu.CompilerParams(vmem_limit_bytes=6 * 2**20),
        cost_estimate=kernel_cost,
    )(starts, lens, keep(query), kv_slots)


def place_kernel(count, window, start_ref, len_ref, *refs):
    in_refs, (out_ref, total) = refs[:count], refs[-2:]
    rows, slot = total.shape[0], in_refs[0].shape[0]
    total[...] = jnp.zeros_like(total)
    row_at = lax.broadcasted_iota(jnp.int32, (window, slot), 0)
    col_at = lax.broadcasted_iota(jnp.int32, (window, slot), 1)
    for s, in_ref in enumerate(in_refs):
        start = start_ref[s]
        first = pl.multiple_of(jnp.minimum((start // 8) * 8, rows - window), 8)
        pick = jnp.where(
            (row_at == col_at + (start - first)) & (col_at < len_ref[s]), 1.0, 0.0
        ).astype(jnp.bfloat16)
        total[pl.ds(first, window), :] += jnp.dot(
            pick, in_ref[...], preferred_element_type=jnp.float32
        )
    out_ref[...] = total[...].astype(out_ref.dtype)


def place(starts, lens, slots, rows, which, all_columns, before):
    count, (slot, columns) = len(slots), slots[0].shape[-2:]
    window = min(rows, slot + 8)
    if isinstance(slots, list):
        in_specs = [pl.BlockSpec((slot, columns), lambda r, a, b: (0, 0))] * count
        operands = list(slots)
    else:
        in_specs = [
            pl.BlockSpec((None, slot, columns), lambda r, a, b, s=s: (s, 0, 0))
            for s in range(count)
        ]
        operands = [slots] * count
    aliases = {}
    if before is not None:
        in_specs.append(pl.BlockSpec(memory_space=pl.ANY))
        operands.append(before)
        aliases = {2 + count: 0}
    grid_spec = pltpu.PrefetchScalarGridSpec(
        num_scalar_prefetch=2,
        grid=(1,),
        in_specs=in_specs,
        out_specs=pl.BlockSpec((rows, columns), lambda r, a, b: (0, which)),
        scratch_shapes=[pltpu.VMEM((rows, columns), jnp.float32)],
    )
    return pl.pallas_call(
        functools.partial(place_kernel, count, window),
        grid_spec=grid_spec,
        out_shape=jax.ShapeDtypeStruct((rows, all_columns), jnp.bfloat16),
        input_output_aliases=aliases,
        compiler_params=pltpu.CompilerParams(vmem_limit_bytes=8 * 2**20),
        cost_estimate=kernel_cost,
    )(starts, lens, *operands)


def local_line(
    rollout_states,
    norm_gain,
    w_query,
    w_key,
    w_value,
    b_query,
    b_key,
    b_value,
    seq_lengths,
    seq_dest,
    seq_offset,
):
    learners = lax.axis_size("dp")
    line = learners // 2
    me = lax.axis_index("dp")
    z, x = me // 2, me % 2
    t = lax.axis_index("tensor")
    row_count, feature_count = rollout_states.shape
    slot = 2 * row_count // learners
    half = feature_count // 2
    middle = row_count // 2

    def after(array, *others):
        return lax.optimization_barrier((array, *others))[0]

    def swap_x(array):
        return lax.ppermute(array, "dp", [(i, i ^ 1) for i in range(learners)])

    def swap_y(array):
        return lax.ppermute(array, "tensor", [(i, i ^ 2) for i in range(4)])

    def swap_core(array):
        return lax.ppermute(array, "tensor", [(i, i ^ 1) for i in range(4)])

    wide = 2 * HD
    along_z = [[2 * i + j for i in range(line)] for j in range(2)]
    groups = [
        [jnp.concatenate([w_key, w_value], axis=1), w_query[:, :wide]],
        [w_query[:, wide : 2 * wide], w_query[:, 2 * wide : 3 * wide]],
        [w_query[:, 3 * wide :]],
    ]
    weights = []
    for group in groups:
        gathered = lax.all_gather(jnp.stack(group), "dp", axis_index_groups=along_z)
        weights.append(pltpu.with_memory_space_constraint(gathered, pltpu.HBM))
    bias_kv = jnp.concatenate([b_key, b_value])[None, :]
    biases = [b_query[None, low : low + wide] for low in range(0, w_query.shape[1], wide)]

    states = rollout_states
    widened = states.astype(jnp.float32)
    squares = jnp.sum(widened * widened, axis=-1)
    squares = squares + swap_core(squares)
    squares = squares + swap_y(squares)
    scale = lax.rsqrt(squares[:, None] / (4 * feature_count) + norm_eps)

    def normed(first):
        part = lax.dynamic_slice_in_dim(states, first, half, 1).astype(jnp.float32)
        gain = lax.dynamic_slice_in_dim(norm_gain, t * feature_count + first, half, 0)
        return (part * scale * gain[None, :]).astype(jnp.bfloat16)

    own, give = normed(x * half), normed((1 - x) * half)

    near_a = swap_x(give[:middle])
    own_a = swap_y(own[:middle])
    own_core = swap_core(own)
    near_b = swap_x(after(give[middle:], near_a))
    diag_a = swap_y(after(near_a, own_a))
    near_a_core = swap_core(near_a)
    own_a_core = swap_core(after(own_a, near_a))
    diag_b = swap_y(after(near_b, diag_a))
    near_b_core = swap_core(after(near_b, diag_a))
    diag_a_core = swap_core(after(diag_a, near_b))
    own_b = swap_y(after(own[middle:], diag_b))
    diag_b_core = swap_core(diag_b)
    near_ax = [[near_a], [near_a_core], [diag_a], [diag_a_core]]
    near_bx = [[near_b], [near_b_core], [diag_b], [diag_b_core]]
    near_x = [pack(near_ax, False), pack(near_bx, False)]
    which = jnp.stack([t ^ i for i in range(4)]).astype(jnp.int32)

    lengths = seq_lengths.reshape(learners, learners)
    dests = seq_dest.reshape(learners, learners)
    offsets = seq_offset.reshape(learners, learners)
    starts = jnp.cumsum(lengths, axis=1) - lengths
    peer_ids = jnp.arange(learners, dtype=jnp.int32)
    rows = jnp.arange(row_count, dtype=jnp.int32)
    length = lax.dynamic_index_in_dim(lengths, me, 0, keepdims=False)
    start = lax.dynamic_index_in_dim(starts, me, 0, keepdims=False)
    dest = lax.dynamic_index_in_dim(dests, me, 0, keepdims=False)
    partners = me ^ peer_ids

    def by_learner(order):
        match = (dest[None, :] == order[:, None]).astype(jnp.int32)
        return jnp.sum(match * start[None, :], axis=1), jnp.sum(match * length[None, :], axis=1)

    send_to = by_learner(partners)
    send_all = by_learner(peer_ids)
    inside = (rows[:, None] >= start[None, :]) & (rows[:, None] < (start + length)[None, :])
    position = rows - jnp.sum(inside.astype(jnp.int32) * start[None, :], axis=1)
    angles = keep(jnp.concatenate(rope_tables(position), axis=1))
    matched = (dests == me).astype(jnp.int32)
    match = (peer_ids[None, :] == partners[:, None]).astype(jnp.int32)
    runs_all = jnp.sum(matched * offsets, axis=1), jnp.sum(matched * lengths, axis=1)
    runs_from = tuple(jnp.sum(match * run[None, :], axis=1) for run in runs_all)

    window = min(row_count, -(-(slot + 16) // 128) * 128)

    def send(outgoing):
        incoming = [outgoing[0]]
        for d in range(1, learners):
            pairs = [(i, i ^ d) for i in range(learners)]
            incoming.append(lax.ppermute(outgoing[d], "dp", pairs))
        return incoming

    def exchange(outgoing):
        return lax.all_to_all(outgoing, "dp", split_axis=0, concat_axis=0, tiled=True)

    def receive(c, incoming, before, *others):
        run_start, run_length = runs_from if isinstance(incoming, list) else runs_all
        start_at = after(run_start, *others)
        return place(start_at, run_length, incoming, row_count, c, w_query.shape[1], before)

    first, second, third = weights
    whole = [(0, wide, jnp.bfloat16)]

    def partial(group, chunks, outs, *others):
        return projection(after(which, *others), near_x, group, chunks, outs)

    def contexts(c, group, chunk, got, others, attend_after=(), apart=False):
        ending = ((True, True), got, biases[c], angles)
        (rot,) = projection(after(which, *others), own_x, group, (chunk,), whole, ending)
        send_start, send_length = send_to if apart else send_all
        start_at = after(send_start, *attend_after)
        slots = kv_slots_to if apart else kv_slots
        return attend(start_at, send_length, rot, slots, window, apart)

    outs = [(0, wide, jnp.float32), (wide, 2 * wide, jnp.bfloat16)]
    part_kv, part_0 = partial(first, (0, 1), outs)
    got_kv = swap_x(part_kv)
    own_b_core = swap_core(after(own_b, part_kv))
    own_x = [keep(pack([[own], [own_core], [own_a, own_b], [own_a_core, own_b_core]], True))]
    got_0 = swap_x(after(part_0, got_kv))
    ending = ((True, False), got_kv, bias_kv, angles)
    (kv,) = projection(which, own_x, first, (0,), whole, ending)
    kv_slots = keep(to_slots(*send_all, kv, slot, window))
    kv_slots_to = keep(to_slots(*send_to, kv, slot, window))
    out_0 = contexts(0, first, 1, got_0, (kv,))
    in_0 = exchange(out_0)
    outs = [(0, wide, jnp.bfloat16), (wide, 2 * wide, jnp.bfloat16)]
    part_1, part_2 = partial(second, (0, 1), outs, out_0)
    got_1 = swap_x(part_1)
    got_2 = swap_x(after(part_2, got_1))
    out_1 = contexts(1, second, 0, got_1, (part_2,), (got_2,))
    in_1 = exchange(out_1)
    (part_3,) = partial(third, (0,), whole, out_1)
    got_3 = swap_x(part_3)
    result = receive(0, in_0, None, part_3)
    out_2 = contexts(2, second, 1, got_2, (part_3,), (got_3,))
    in_2 = exchange(after(out_2, in_0))
    out_3 = contexts(3, third, 0, got_3, (out_2,), apart=True)
    in_3 = send(out_3)
    result = receive(1, in_1, result, out_3[0])
    result = receive(2, in_2, result, out_3[0])
    return receive(3, in_3, result)


def solution(mesh):
    placed = (
        P("dp", "tensor"),
        P(),
        P("dp", "tensor"),
        P("dp", "tensor"),
        P("dp", "tensor"),
        P("tensor"),
        P("tensor"),
        P("tensor"),
        P(),
        P(),
        P(),
    )
    fits_line = mesh.shape["dp"] == 8 and mesh.shape["tensor"] == 4
    return jax.shard_map(
        local_line if fits_line else local_any,
        mesh=mesh,
        in_specs=placed,
        out_specs=P("dp", "tensor"),
        check_vma=False,
    )
```

profile of v0, /device:TPU:0, one launch (start us, length us, event | category | flops | bytes accessed | tf_op | source)
XLA Modules:
  0.0 339.3 jit_solution(7969496090832709638)
XLA Ops:
  11.4 3.1 multiply_reduce_fusion
  20.3 3.5 %multiply_convert_fusion = (bf16[1024,1024]{1,0:T(8,128)(2,1)S(1)}, bf16[1024,1024]{1,0:T(8,128)(2,1)S(1)}) fusion(f32[1024]{0:T(1024)S(1)} %get-tuple-element.87, bf16[1024,2048]{1,0:T(8,128)(2,1)} %param.11, s32[]{:T(128)S(6)} %select_n.29, f32[1024]{0:T(1024)S(1)} %add_rsqrt_fusion, f32[1024]{0:T(1024)S(1)} %get-tuple-element.88, s32[]{:T(128)S(6)} %select_n.27), kind=kLoop, calls=%fused_computation.1 | loop fusion | flops 8388608 | bytes 8400904 | tf_op jit(solution)/shard_map/convert_element_type | solution.py:473
  28.8 20.8 %collective-permute-done.3.refs_2_ = bf16[512,1024]{1,0:T(8,128)(2,1)S(1)} collective-permute-done((bf16[512,1024]{1,0:T(8,128)(2,1)S(1)}, bf16[512,1024]{1,0:T(8,128)(2,1)S(1)}, u32[]{:S(2)}, u32[]{:S(2)}) %collective-permute-start.3) | collective-permute-done | bytes 1048608 | tf_op jit(solution)/shard_map/ppermute | solution.py:444
  53.4 21.3 %collective-permute-done.6.refs_2_ = bf16[512,1024]{1,0:T(8,128)(2,1)} collective-permute-done((bf16[512,1024]{1,0:T(8,128)(2,1)}, bf16[512,1024]{1,0:T(8,128)(2,1)}, u32[]{:S(2)}, u32[]{:S(2)}) %collective-permute-start.6) | collective-permute-done | bytes 1048608 | tf_op jit(solution)/shard_map/ppermute | solution.py:444
  77.3 19.9 %collective-permute-done.7.refs_2_ = bf16[512,1024]{1,0:T(8,128)(2,1)} collective-permute-done((bf16[512,1024]{1,0:T(8,128)(2,1)}, bf16[512,1024]{1,0:T(8,128)(2,1)}, u32[]{:S(2)}, u32[]{:S(2)}) %collective-permute-start.7) | collective-permute-done | bytes 1048608 | tf_op jit(solution)/shard_map/ppermute | solution.py:444
  112.5 7.3 %shard_map.111 = (f32[1024,256]{1,0:T(8,128)S(1)}, bf16[1024,256]{1,0:T(8,128)(2,1)S(1)}) custom-call(s32[4]{0:T(128)S(1)} %pad_add_fusion.which_ref, bf16[4,512,1024]{2,1,0:T(8,128)(2,1)S(1)} %copy-done.14, bf16[4,512,1024]{2,1,0:T(8,128)(2,1)S(1)} %copy-done.18, bf16[4,2,1024,256]{3,2,1,0:T(8,128)(2,1)} %bitcast.36), custom_call_target="tpu_custom_call" | custom-call | flops 4000000000 | bytes 1048576 | tf_op jit(solution)/shard_map/pallas_call | solution.py:257
  126.4 18.7 %collective-permute-done.15.refs_2_ = f32[1024,256]{1,0:T(8,128)S(1)} collective-permute-done((f32[1024,256]{1,0:T(8,128)S(1)}, f32[1024,256]{1,0:T(8,128)S(1)}, u32[]{:S(2)}, u32[]{:S(2)}) %collective-permute-start.15) | collective-permute-done | bytes 1048608 | tf_op jit(solution)/shard_map/ppermute | solution.py:441
  148.9 6.3 %shard_map.113.in_ref = bf16[1024,256]{1,0:T(8,128)(2,1)S(1)} custom-call(s32[4]{0:T(128)S(1)} %pad_add_fusion.which_ref, bf16[4,1024,1024]{2,1,0:T(8,128)(2,1)S(1)} %shard_map.112.refs_0_, bf16[4,2,1024,256]{3,2,1,0:T(8,128)(2,1)} %bitcast.37, f32[1024,256]{1,0:T(8,128)S(1)} %collective-permute-done.15.refs_2_, f32[1,256]{1,0:T(1,128)S(1)} %bitcast.28, ...), custom_call_target="tpu_custom_call" | custom-call | flops 4000000000 | bytes 1048576 | tf_op jit(solution)/shard_map/pallas_call | solution.py:257
  158.3 4.8 %shard_map.114.q_ref = bf16[1024,256]{1,0:T(8,128)(2,1)S(1)} custom-call(s32[4]{0:T(128)S(1)} %pad_add_fusion.which_ref, bf16[4,1024,1024]{2,1,0:T(8,128)(2,1)S(1)} %shard_map.112.refs_0_, bf16[4,2,1024,256]{3,2,1,0:T(8,128)(2,1)} %bitcast.38, bf16[1024,256]{1,0:T(8,128)(2,1)S(1)} %collective-permute-done.16.refs_2_, f32[1,256]{1,0:T(1,128)S(1)} %bitcast.32, ...), custom_call_target="tpu_custom_call" | custom-call | flops 4000000000 | bytes 1048576 | tf_op jit(solution)/shard_map/pallas_call | solution.py:257
  163.1 7.6 %shard_map.116 = bf16[8,256,256]{2,1,0:T(8,128)(2,1)} custom-call(s32[8]{0:T(128)S(1)} %get-tuple-element.55.start_ref, s32[8]{0:T(128)S(1)} %get-tuple-element.69.len_ref, bf16[1024,256]{1,0:T(8,128)(2,1)S(1)} %shard_map.114.q_ref, bf16[8,256,256]{2,1,0:T(8,128)(2,1)S(1)} %shard_map.115.kv_ref), custom_call_target="tpu_custom_call" | custom-call | flops 4000000000 | bytes 1048576 | tf_op jit(solution)/shard_map/pallas_call | solution.py:348
  170.7 6.0 %all-to-all-start = ((bf16[8,256,256]{2,1,0:T(8,128)(2,1)}), bf16[8,256,256]{2,1,0:T(8,128)(2,1)S(1)}, u32[]{:S(2)}, u32[]{:S(2)}) async-start(bf16[8,256,256]{2,1,0:T(8,128)(2,1)} %shard_map.116), calls=%async_computation | async-start | bytes 2097152 | tf_op jit(solution)/shard_map/all_to_all | solution.py:529
  181.1 7.5 %shard_map.117 = (bf16[1024,256]{1,0:T(8,128)(2,1)S(1)}, bf16[1024,256]{1,0:T(8,128)(2,1)S(1)}) custom-call(s32[4]{0:T(128)S(1)} %pad_add_fusion.which_ref, bf16[4,512,1024]{2,1,0:T(8,128)(2,1)S(1)} %copy-done.15, bf16[4,512,1024]{2,1,0:T(8,128)(2,1)S(1)} %copy-done.19, bf16[4,2,1024,256]{3,2,1,0:T(8,128)(2,1)} %bitcast.33), custom_call_target="tpu_custom_call" | custom-call | flops 4000000000 | bytes 1048576 | tf_op jit(solution)/shard_map/pallas_call | solution.py:257
  190.7 13.2 %collective-permute-done.17.refs_2_ = bf16[1024,256]{1,0:T(8,128)(2,1)S(1)} collective-permute-done((bf16[1024,256]{1,0:T(8,128)(2,1)S(1)}, bf16[1024,256]{1,0:T(8,128)(2,1)S(1)}, u32[]{:S(2)}, u32[]{:S(2)}) %collective-permute-start.17) | collective-permute-done | bytes 524320 | tf_op jit(solution)/shard_map/ppermute | solution.py:441
  203.9 3.4 copy-done.1
  207.3 4.8 %shard_map.118.q_ref = bf16[1024,256]{1,0:T(8,128)(2,1)S(1)} custom-call(s32[4]{0:T(128)S(1)} %pad_add_fusion.which_ref, bf16[4,1024,1024]{2,1,0:T(8,128)(2,1)S(1)} %copy-done.1, bf16[4,2,1024,256]{3,2,1,0:T(8,128)(2,1)} %bitcast.34, bf16[1024,256]{1,0:T(8,128)(2,1)S(1)} %collective-permute-done.17.refs_2_, f32[1,256]{1,0:T(1,128)S(1)} %bitcast.31, ...), custom_call_target="tpu_custom_call" | custom-call | flops 4000000000 | bytes 1048576 | tf_op jit(solution)/shard_map/pallas_call | solution.py:257
  212.0 3.5 %collective-permute-done.18.refs_2_ = bf16[1024,256]{1,0:T(8,128)(2,1)S(1)} collective-permute-done((bf16[1024,256]{1,0:T(8,128)(2,1)S(1)}, bf16[1024,256]{1,0:T(8,128)(2,1)S(1)}, u32[]{:S(2)}, u32[]{:S(2)}) %collective-permute-start.18) | collective-permute-done | bytes 524320 | tf_op jit(solution)/shard_map/ppermute | solution.py:441
  215.5 7.6 %shard_map.119 = bf16[8,256,256]{2,1,0:T(8,128)(2,1)} custom-call(s32[8]{0:T(128)S(1)} %get-tuple-element.55.start_ref, s32[8]{0:T(128)S(1)} %get-tuple-element.69.len_ref, bf16[1024,256]{1,0:T(8,128)(2,1)S(1)} %shard_map.118.q_ref, bf16[8,256,256]{2,1,0:T(8,128)(2,1)S(1)} %copy-done.22), custom_call_target="tpu_custom_call" | custom-call | flops 4000000000 | bytes 1048576 | tf_op jit(solution)/shard_map/pallas_call | solution.py:348
  223.1 6.2 %all-to-all-start.2 = ((bf16[8,256,256]{2,1,0:T(8,128)(2,1)}), bf16[8,256,256]{2,1,0:T(8,128)(2,1)S(1)}, u32[]{:S(2)}, u32[]{:S(2)}) async-start(bf16[8,256,256]{2,1,0:T(8,128)(2,1)} %shard_map.119), calls=%async_computation.2 | async-start | bytes 2097152 | tf_op jit(solution)/shard_map/all_to_all | solution.py:529
  229.3 20.9 %all-gather.11.cloned.1.call-done = bf16[4096,256]{1,0:T(8,128)(2,1)} async-done(((bf16[1024,256]{1,0:T(8,128)(2,1)}), bf16[4096,256]{1,0:T(8,128)(2,1)}) %all-gather.11.cloned.1.call-update) | async-done | bytes 2097168 | tf_op jit(solution)/shard_map/all_gather | solution.py:458
  254.6 4.4 %shard_map.120 = bf16[1024,256]{1,0:T(8,128)(2,1)S(1)} custom-call(s32[4]{0:T(128)S(1)} %pad_add_fusion.which_ref, bf16[4,512,1024]{2,1,0:T(8,128)(2,1)S(1)} %copy-done.16, bf16[4,512,1024]{2,1,0:T(8,128)(2,1)S(1)} %copy-done.20, bf16[4,1,1024,256]{3,2,1,0:T(8,128)(2,1)} %bitcast.39), custom_call_target="tpu_custom_call" | custom-call | flops 4000000000 | bytes 1048576 | tf_op jit(solution)/shard_map/pallas_call | solution.py:257
  260.3 3.4 copy-done.2
  263.7 4.8 %shard_map.121.q_ref = bf16[1024,256]{1,0:T(8,128)(2,1)S(1)} custom-call(s32[4]{0:T(128)S(1)} %pad_add_fusion.which_ref, bf16[4,1024,1024]{2,1,0:T(8,128)(2,1)S(1)} %copy-done.2, bf16[4,2,1024,256]{3,2,1,0:T(8,128)(2,1)} %bitcast.35, bf16[1024,256]{1,0:T(8,128)(2,1)S(1)} %collective-permute-done.18.refs_2_, f32[1,256]{1,0:T(1,128)S(1)} %bitcast.30, ...), custom_call_target="tpu_custom_call" | custom-call | flops 4000000000 | bytes 1048576 | tf_op jit(solution)/shard_map/pallas_call | solution.py:257
  268.4 4.5 %collective-permute-done.19.refs_2_ = bf16[1024,256]{1,0:T(8,128)(2,1)S(1)} collective-permute-done((bf16[1024,256]{1,0:T(8,128)(2,1)S(1)}, bf16[1024,256]{1,0:T(8,128)(2,1)S(1)}, u32[]{:S(2)}, u32[]{:S(2)}) %collective-permute-start.19) | collective-permute-done | bytes 524320 | tf_op jit(solution)/shard_map/ppermute | solution.py:441
  273.7 7.6 %shard_map.122 = bf16[8,256,256]{2,1,0:T(8,128)(2,1)} custom-call(s32[8]{0:T(128)S(1)} %get-tuple-element.55.start_ref, s32[8]{0:T(128)S(1)} %get-tuple-element.69.len_ref, bf16[1024,256]{1,0:T(8,128)(2,1)S(1)} %shard_map.121.q_ref, bf16[8,256,256]{2,1,0:T(8,128)(2,1)S(1)} %copy-done.23), custom_call_target="tpu_custom_call" | custom-call | flops 4000000000 | bytes 1048576 | tf_op jit(solution)/shard_map/pallas_call | solution.py:348
  281.3 3.8 %all-to-all-start.1 = ((bf16[8,256,256]{2,1,0:T(8,128)(2,1)}), bf16[8,256,256]{2,1,0:T(8,128)(2,1)S(1)}, u32[]{:S(2)}, u32[]{:S(2)}) async-start(bf16[8,256,256]{2,1,0:T(8,128)(2,1)} %shard_map.122), calls=%async_computation.1 | async-start | bytes 2097152 | tf_op jit(solution)/shard_map/all_to_all | solution.py:529
  287.5 3.4 copy-done.3
  290.9 4.7 %shard_map.123.q_ref = bf16[1024,256]{1,0:T(8,128)(2,1)S(1)} custom-call(s32[4]{0:T(128)S(1)} %pad_add_fusion.which_ref, bf16[4,1024,1024]{2,1,0:T(8,128)(2,1)S(1)} %copy-done.3, bf16[4,1,1024,256]{3,2,1,0:T(8,128)(2,1)} %bitcast.40, bf16[1024,256]{1,0:T(8,128)(2,1)S(1)} %copy-done.8, f32[1,256]{1,0:T(1,128)S(1)} %bitcast.29, f32[1024,128]{1,0:T(8,128)S(1)} %copy-done.6), custom_call_target="tpu_custom_call" | custom-call | flops 4000000000 | bytes 1048576 | tf_op jit(solution)/shard_map/pallas_call | solution.py:257
  295.6 6.6 %shard_map.125 = (bf16[256,256]{1,0:T(8,128)(2,1)S(1)}, bf16[256,256]{1,0:T(8,128)(2,1)S(1)}, bf16[256,256]{1,0:T(8,128)(2,1)S(1)}, bf16[256,256]{1,0:T(8,128)(2...) custom-call(s32[8]{0:T(128)S(1)} %get-tuple-element.71.start_ref, ...), custom_call_target="tpu_custom_call" | custom-call | flops 4000000000 | bytes 1048576 | tf_op jit(solution)/shard_map/pallas_call | solution.py:348
  314.6 3.3 collective-permute-start.25
  320.6 5.9 %collective-permute-done.23.refs_4_ = bf16[256,256]{1,0:T(8,128)(2,1)} collective-permute-done((bf16[256,256]{1,0:T(8,128)(2,1)}, bf16[256,256]{1,0:T(8,128)(2,1)}, u32[]{:S(2)}, u32[]{:S(2)}) %collective-permute-start.23) | collective-permute-done | bytes 131104 | tf_op jit(solution)/shard_map/ppermute | solution.py:525
  326.4 3.1 collective-permute-done.24.refs_5_
  329.5 3.0 shard_map.129
  (153 shorter events, 80.9 us)
Async XLA Ops:
  6.5 101.6 %all-gather.7.cloned.1.call-start = ((), (), s32[]{:S(2)}) async-start(), calls=%async_computation.3 | async-start | bytes 5242880 | tf_op jit(solution)/shard_map/all_gather | solution.py:458
  10.3 166.4 %all-gather.9.cloned.1.call-start = ((), (), s32[]{:S(2)}) async-start(), calls=%async_computation.4 | async-start | bytes 5242880 | tf_op jit(solution)/shard_map/all_gather | solution.py:458
  11.4 238.8 %all-gather.11.cloned.1.call-start = ((), (), s32[]{:S(2)}) async-start(), calls=%async_computation.5 | async-start | bytes 2621440 | tf_op jit(solution)/shard_map/all_gather | solution.py:458
  15.9 4.4 %collective-permute-start.1 = (f32[1024]{0:T(1024)S(1)}, f32[1024]{0:T(1024)S(1)}, u32[]{:S(2)}, u32[]{:S(2)}) collective-permute-start(f32[1024]{0:T(1024)S(1)} %add.48), channel_id=1, source_target_pairs={{0,2},{1,3},{2,0},{3,1},{4,6},{5,7},{6,4},{7,5},{8,10},{9,11},{10,... | collective-permute-start | bytes 12296 | tf_op jit(solution)/shard_map/ppermute | solution.py:444
  25.1 24.5 %collective-permute-start.3 = (bf16[512,1024]{1,0:T(8,128)(2,1)S(1)}, bf16[512,1024]{1,0:T(8,128)(2,1)S(1)}, u32[]{:S(2)}, u32[]{:S(2)}) collective-permute-start(bf16[512,1024]{1,0:T(8,128)(2,1)S(1)} %get-tuple-element.86), channel_id=1, source_target_pairs={{0,2},{1,3},{2,0},{3,1},{4,6},{5,7},{6,4},{7,5},{8,10},{9,11},{10,... | collective-permute-start | bytes 3145736 | tf_op jit(solution)/shard_map/ppermute | solution.py:444
  27.3 24.1 %collective-permute-start.4 = (bf16[512,1024]{1,0:T(8,128)(2,1)S(1)}, bf16[512,1024]{1,0:T(8,128)(2,1)}, u32[]{:S(2)}, u32[]{:S(2)}) collective-permute-start(bf16[512,1024]{1,0:T(8,128)(2,1)S(1)} %get-tuple-element.83), channel_id=1, source_target_pairs={{0,4},{4,0},{8,12},{12,8},{16,20},{20,16},{24,28},{28,24},{1,5},{5... | collective-permute-start | bytes 3145736 | tf_op jit(solution)/shard_map/ppermute | solution.py:441
  51.4 23.3 %collective-permute-start.6 = (bf16[512,1024]{1,0:T(8,128)(2,1)}, bf16[512,1024]{1,0:T(8,128)(2,1)}, u32[]{:S(2)}, u32[]{:S(2)}) collective-permute-start(bf16[512,1024]{1,0:T(8,128)(2,1)} %collective-permute-done.4.refs_0_), channel_id=1, source_target_pairs={{0,2},{1,3},{2,0},{3,1},{4,6},{5,7},{6,4},{7,5},{8,10},{9,11},{10,... | collective-permute-start | bytes 3145736 | tf_op jit(solution)/shard_map/ppermute | solution.py:444
  51.7 23.1 %collective-permute-start.5 = (bf16[512,1024]{1,0:T(8,128)(2,1)S(1)}, bf16[512,1024]{1,0:T(8,128)(2,1)}, u32[]{:S(2)}, u32[]{:S(2)}) collective-permute-start(bf16[512,1024]{1,0:T(8,128)(2,1)S(1)} %get-tuple-element.37), channel_id=1, source_target_pairs={{0,4},{4,0},{8,12},{12,8},{16,20},{20,16},{24,28},{28,24},{1,5},{5... | collective-permute-start | bytes 3145736 | tf_op jit(solution)/shard_map/ppermute | solution.py:441
  74.8 22.4 %collective-permute-start.7 = (bf16[512,1024]{1,0:T(8,128)(2,1)}, bf16[512,1024]{1,0:T(8,128)(2,1)}, u32[]{:S(2)}, u32[]{:S(2)}) collective-permute-start(bf16[512,1024]{1,0:T(8,128)(2,1)} %collective-permute-done.5.refs_0_), channel_id=1, source_target_pairs={{0,2},{1,3},{2,0},{3,1},{4,6},{5,7},{6,4},{7,5},{8,10},{9,11},{10,... | collective-permute-start | bytes 3145736 | tf_op jit(solution)/shard_map/ppermute | solution.py:444
  76.2 22.0 %collective-permute-start.10 = (bf16[512,1024]{1,0:T(8,128)(2,1)}, bf16[512,1024]{1,0:T(8,128)(2,1)}, u32[]{:S(2)}, u32[]{:S(2)}) collective-permute-start(bf16[512,1024]{1,0:T(8,128)(2,1)} %collective-permute-done.4.refs_0_), channel_id=1, source_target_pairs={{0,1},{1,0},{2,3},{3,2},{4,5},{5,4},{6,7},{7,6},{8,9},{9,8},{10,11... | collective-permute-start | bytes 3145736 | tf_op jit(solution)/shard_map/ppermute | solution.py:447
  76.2 22.1 %collective-permute-start.11 = (bf16[512,1024]{1,0:T(8,128)(2,1)}, bf16[512,1024]{1,0:T(8,128)(2,1)}, u32[]{:S(2)}, u32[]{:S(2)}) collective-permute-start(bf16[512,1024]{1,0:T(8,128)(2,1)} %collective-permute-done.6.refs_2_), channel_id=1, source_target_pairs={{0,1},{1,0},{2,3},{3,2},{4,5},{5,4},{6,7},{7,6},{8,9},{9,8},{10,11... | collective-permute-start | bytes 3145736 | tf_op jit(solution)/shard_map/ppermute | solution.py:447
  77.3 26.9 %collective-permute-start.12 = (bf16[512,1024]{1,0:T(8,128)(2,1)}, bf16[512,1024]{1,0:T(8,128)(2,1)S(1)}, u32[]{:S(2)}, u32[]{:S(2)}) collective-permute-start(bf16[512,1024]{1,0:T(8,128)(2,1)} %collective-permute-done.5.refs_0_), channel_id=1, source_target_pairs={{0,1},{1,0},{2,3},{3,2},{4,5},{5,4},{6,7},{7,6},{8,9},{9,8},{10,11... | collective-permute-start | bytes 3145736 | tf_op jit(solution)/shard_map/ppermute | solution.py:447
  97.2 6.9 %collective-permute-start.13 = (bf16[512,1024]{1,0:T(8,128)(2,1)}, bf16[512,1024]{1,0:T(8,128)(2,1)S(1)}, u32[]{:S(2)}, u32[]{:S(2)}) collective-permute-start(bf16[512,1024]{1,0:T(8,128)(2,1)} %collective-permute-done.7.refs_2_), channel_id=1, source_target_pairs={{0,1},{1,0},{2,3},{3,2},{4,5},{5,4},{6,7},{7,6},{8,9},{9,8},{10,11... | collective-permute-start | bytes 3145736 | tf_op jit(solution)/shard_map/ppermute | solution.py:447
  97.6 48.8 %collective-permute-start.2 = (bf16[1024,1024]{1,0:T(8,128)(2,1)S(1)}, bf16[1024,1024]{1,0:T(8,128)(2,1)}, u32[]{:S(2)}, u32[]{:S(2)}) collective-permute-start(bf16[1024,1024]{1,0:T(8,128)(2,1)S(1)} %get-tuple-element.78.refs_0_), channel_id=1, source_target_pairs={{0,1},{1,0},{2,3},{3,2},{4,5},{5,4},{6,7},{7,6},{8,9},{9,8},{10,11... | collective-permute-start | bytes 6291464 | tf_op jit(solution)/shard_map/ppermute | solution.py:447
  98.2 48.3 %collective-permute-start.9 = (bf16[512,1024]{1,0:T(8,128)(2,1)S(1)}, bf16[512,1024]{1,0:T(8,128)(2,1)}, u32[]{:S(2)}, u32[]{:S(2)}) collective-permute-start(bf16[512,1024]{1,0:T(8,128)(2,1)S(1)} %collective-permute-done.3.refs_2_), channel_id=1, source_target_pairs={{0,1},{1,0},{2,3},{3,2},{4,5},{5,4},{6,7},{7,6},{8,9},{9,8},{10,11... | collective-permute-start | bytes 3145736 | tf_op jit(solution)/shard_map/ppermute | solution.py:447
  98.3 25.8 %collective-permute-start.8 = (bf16[512,1024]{1,0:T(8,128)(2,1)}, bf16[512,1024]{1,0:T(8,128)(2,1)}, u32[]{:S(2)}, u32[]{:S(2)}) collective-permute-start(bf16[512,1024]{1,0:T(8,128)(2,1)} %get-tuple-element.40), channel_id=1, source_target_pairs={{0,2},{1,3},{2,0},{3,1},{4,6},{5,7},{6,4},{7,5},{8,10},{9,11},{10,... | collective-permute-start | bytes 3145736 | tf_op jit(solution)/shard_map/ppermute | solution.py:444
  119.8 25.3 %collective-permute-start.15 = (f32[1024,256]{1,0:T(8,128)S(1)}, f32[1024,256]{1,0:T(8,128)S(1)}, u32[]{:S(2)}, u32[]{:S(2)}) collective-permute-start(f32[1024,256]{1,0:T(8,128)S(1)} %get-tuple-element.43), channel_id=1, source_target_pairs={{0,4},{4,0},{8,12},{12,8},{16,20},{20,16},{24,28},{28,24},{1,5},{5... | collective-permute-start | bytes 3145736 | tf_op jit(solution)/shard_map/ppermute | solution.py:441
  124.1 22.4 %collective-permute-start.14 = (bf16[512,1024]{1,0:T(8,128)(2,1)}, bf16[512,1024]{1,0:T(8,128)(2,1)S(1)}, u32[]{:S(2)}, u32[]{:S(2)}) collective-permute-start(bf16[512,1024]{1,0:T(8,128)(2,1)} %collective-permute-done.8.refs_3_), channel_id=1, source_target_pairs={{0,1},{1,0},{2,3},{3,2},{4,5},{5,4},{6,7},{7,6},{8,9},{9,8},{10,11... | collective-permute-start | bytes 3145736 | tf_op jit(solution)/shard_map/ppermute | solution.py:447
  145.1 13.3 %collective-permute-start.16 = (bf16[1024,256]{1,0:T(8,128)(2,1)S(1)}, bf16[1024,256]{1,0:T(8,128)(2,1)S(1)}, u32[]{:S(2)}, u32[]{:S(2)}) collective-permute-start(bf16[1024,256]{1,0:T(8,128)(2,1)S(1)} %get-tuple-element.47), channel_id=1, source_target_pairs={{0,4},{4,0},{8,12},{12,8},{16,20},{20,16},{24,28},{28,24},{1,5},{5... | collective-permute-start | bytes 1572872 | tf_op jit(solution)/shard_map/ppermute | solution.py:441
  170.7 52.4 %all-to-all-start = ((bf16[8,256,256]{2,1,0:T(8,128)(2,1)}), bf16[8,256,256]{2,1,0:T(8,128)(2,1)S(1)}, u32[]{:S(2)}, u32[]{:S(2)}) async-start(bf16[8,256,256]{2,1,0:T(8,128)(2,1)} %shard_map.116), calls=%async_computation | async-start | bytes 2097152 | tf_op jit(solution)/shard_map/all_to_all | solution.py:529
  188.6 15.3 %collective-permute-start.17 = (bf16[1024,256]{1,0:T(8,128)(2,1)S(1)}, bf16[1024,256]{1,0:T(8,128)(2,1)S(1)}, u32[]{:S(2)}, u32[]{:S(2)}) collective-permute-start(bf16[1024,256]{1,0:T(8,128)(2,1)S(1)} %get-tuple-element.50), channel_id=1, source_target_pairs={{0,4},{4,0},{8,12},{12,8},{16,20},{20,16},{24,28},{28,24},{1,5},{5... | collective-permute-start | bytes 1572872 | tf_op jit(solution)/shard_map/ppermute | solution.py:441
  203.9 11.6 %collective-permute-start.18 = (bf16[1024,256]{1,0:T(8,128)(2,1)S(1)}, bf16[1024,256]{1,0:T(8,128)(2,1)S(1)}, u32[]{:S(2)}, u32[]{:S(2)}) collective-permute-start(bf16[1024,256]{1,0:T(8,128)(2,1)S(1)} %get-tuple-element.51), channel_id=1, source_target_pairs={{0,4},{4,0},{8,12},{12,8},{16,20},{20,16},{24,28},{28,24},{1,5},{5... | collective-permute-start | bytes 1572872 | tf_op jit(solution)/shard_map/ppermute | solution.py:441
  223.1 58.2 %all-to-all-start.2 = ((bf16[8,256,256]{2,1,0:T(8,128)(2,1)}), bf16[8,256,256]{2,1,0:T(8,128)(2,1)S(1)}, u32[]{:S(2)}, u32[]{:S(2)}) async-start(bf16[8,256,256]{2,1,0:T(8,128)(2,1)} %shard_map.119), calls=%async_computation.2 | async-start | bytes 2097152 | tf_op jit(solution)/shard_map/all_to_all | solution.py:529
  259.0 14.0 %collective-permute-start.19 = (bf16[1024,256]{1,0:T(8,128)(2,1)S(1)}, bf16[1024,256]{1,0:T(8,128)(2,1)S(1)}, u32[]{:S(2)}, u32[]{:S(2)}) collective-permute-start(bf16[1024,256]{1,0:T(8,128)(2,1)S(1)} %shard_map.120), channel_id=1, source_target_pairs={{0,4},{4,0},{8,12},{12,8},{16,20},{20,16},{24,28},{28,24},{1,5},{5... | collective-permute-start | bytes 1572872 | tf_op jit(solution)/shard_map/ppermute | solution.py:441
  281.3 37.3 %all-to-all-start.1 = ((bf16[8,256,256]{2,1,0:T(8,128)(2,1)}), bf16[8,256,256]{2,1,0:T(8,128)(2,1)S(1)}, u32[]{:S(2)}, u32[]{:S(2)}) async-start(bf16[8,256,256]{2,1,0:T(8,128)(2,1)} %shard_map.122), calls=%async_computation.1 | async-start | bytes 2097152 | tf_op jit(solution)/shard_map/all_to_all | solution.py:529
  302.9 11.7 %collective-permute-start.20 = (bf16[256,256]{1,0:T(8,128)(2,1)S(1)}, bf16[256,256]{1,0:T(8,128)(2,1)S(1)}, u32[]{:S(2)}, u32[]{:S(2)}) collective-permute-start(bf16[256,256]{1,0:T(8,128)(2,1)S(1)} %get-tuple-element.59), channel_id=1, source_target_pairs={{0,4},{4,0},{8,12},{12,8},{16,20},{20,16},{24,28},{28,24},{1,5},{5... | collective-permute-start | bytes 393224 | tf_op jit(solution)/shard_map/ppermute | solution.py:525
  304.9 13.0 %collective-permute-start.21 = (bf16[256,256]{1,0:T(8,128)(2,1)S(1)}, bf16[256,256]{1,0:T(8,128)(2,1)S(1)}, u32[]{:S(2)}, u32[]{:S(2)}) collective-permute-start(bf16[256,256]{1,0:T(8,128)(2,1)S(1)} %get-tuple-element.60), channel_id=1, source_target_pairs={{0,8},{4,12},{8,0},{12,4},{16,24},{20,28},{24,16},{28,20},{1,9},{5... | collective-permute-start | bytes 393224 | tf_op jit(solution)/shard_map/ppermute | solution.py:525
  306.3 14.2 %collective-permute-start.22 = (bf16[256,256]{1,0:T(8,128)(2,1)}, bf16[256,256]{1,0:T(8,128)(2,1)}, u32[]{:S(2)}, u32[]{:S(2)}) collective-permute-start(bf16[256,256]{1,0:T(8,128)(2,1)} %get-tuple-element.61), channel_id=1, source_target_pairs={{0,12},{4,8},{8,4},{12,0},{16,28},{20,24},{24,20},{28,16},{1,13},{... | collective-permute-start | bytes 393224 | tf_op jit(solution)/shard_map/ppermute | solution.py:525
  306.4 20.0 %collective-permute-start.23 = (bf16[256,256]{1,0:T(8,128)(2,1)}, bf16[256,256]{1,0:T(8,128)(2,1)}, u32[]{:S(2)}, u32[]{:S(2)}) collective-permute-start(bf16[256,256]{1,0:T(8,128)(2,1)} %get-tuple-element.62), channel_id=1, source_target_pairs={{0,16},{4,20},{8,24},{12,28},{16,0},{20,4},{24,8},{28,12},{1,17},{... | collective-permute-start | bytes 393224 | tf_op jit(solution)/shard_map/ppermute | solution.py:525
  309.3 20.2 %collective-permute-start.24 = (bf16[256,256]{1,0:T(8,128)(2,1)}, bf16[256,256]{1,0:T(8,128)(2,1)}, u32[]{:S(2)}, u32[]{:S(2)}) collective-permute-start(bf16[256,256]{1,0:T(8,128)(2,1)} %get-tuple-element.63), channel_id=1, source_target_pairs={{0,20},{4,16},{8,28},{12,24},{16,4},{20,0},{24,12},{28,8},{1,21},{... | collective-permute-start | bytes 393224 | tf_op jit(solution)/shard_map/ppermute | solution.py:525
  314.6 14.9 %collective-permute-start.25 = (bf16[256,256]{1,0:T(8,128)(2,1)}, bf16[256,256]{1,0:T(8,128)(2,1)S(1)}, u32[]{:S(2)}, u32[]{:S(2)}) collective-permute-start(bf16[256,256]{1,0:T(8,128)(2,1)} %get-tuple-element.64), channel_id=1, source_target_pairs={{0,24},{4,28},{8,16},{12,20},{16,8},{20,12},{24,0},{28,4},{1,25},{... | collective-permute-start | bytes 393224 | tf_op jit(solution)/shard_map/ppermute | solution.py:525
  318.5 11.0 %collective-permute-start.26 = (bf16[256,256]{1,0:T(8,128)(2,1)S(1)}, bf16[256,256]{1,0:T(8,128)(2,1)S(1)}, u32[]{:S(2)}, u32[]{:S(2)}) collective-permute-start(bf16[256,256]{1,0:T(8,128)(2,1)S(1)} %get-tuple-element.65), channel_id=1, source_target_pairs={{0,28},{4,24},{8,20},{12,16},{16,12},{20,8},{24,4},{28,0},{1,29},{... | collective-permute-start | bytes 393224 | tf_op jit(solution)/shard_map/ppermute | solution.py:525
  (35 other events, 472.5 us)
Sparse Core Ops, SparseCore 0:
  10.4 83.4 all-gather.6
  95.4 79.2 all-gather.8
  176.3 73.7 all-gather.10
where the time goes:
time: 346 us; the launch traced here: 339 us
  waiting for transfers between devices  140 us (40%)
  Pallas kernels  92.3 us (27%)
  starting transfers between devices  46.3 us (13%)
  local copies, waits for them, and re-layouts  35.3 us (10%)
  between operations  13.8 us (4%)
  other arithmetic  11.7 us (3%)
    ppermute x5, waiting for transfers between devices, swap_y(): return lax.ppermute(array, 'tensor', [(i, i ^ 2) for i in range(4)])  65.7 us
    pallas_call x8, Pallas kernels, projection(): pl.pallas_call(functools.partial(product_kernel, len(x_parts), ropes, tup...  44.6 us
    ppermute x7, waiting for transfers between devices, swap_x(): return lax.ppermute(array, 'dp', [(i, i ^ 1) for i in range(learners)])  43.4 us
    unnamed x68, local copies, waits for them, and re-layouts  30.5 us
    pallas_call x4, Pallas kernels, attend(): pl.pallas_call(functools.partial(attend_kernel, columns // HD, window), i...  29.4 us
    all_gather x3, waiting for transfers between devices, local_line(): gathered = lax.all_gather(jnp.stack(group), 'dp', axis_index_groups=along_z)  20.9 us
    all_to_all x3, starting transfers between devices, exchange(): lax.all_to_all(outgoing, 'dp', split_axis=0, concat_axis=0, tiled=True)  16 us
    ppermute x7, starting transfers between devices, send(): incoming.append(lax.ppermute(outgoing[d], 'dp', pairs))  11.2 us
  transfers between devices with their start and end apart: 33, of which 16 were waited for; matrix products, arithmetic and copies ran while one was open for 4% of the time, Pallas kernels for 26%

commit v1 on v0

--- a/solution.py
+++ b/solution.py
@@ -565,11 +565,11 @@
     got_2 = swap_x(after(part_2, got_1))
     out_1 = contexts(1, second, 0, got_1, (part_2,), (got_2,))
     in_1 = exchange(out_1)
-    (part_3,) = partial(third, (0,), whole, out_1)
+    out_2 = contexts(2, second, 1, got_2, (out_1,))
+    (part_3,) = partial(third, (0,), whole, out_2)
     got_3 = swap_x(part_3)
     result = receive(0, in_0, None, part_3)
-    out_2 = contexts(2, second, 1, got_2, (part_3,), (got_3,))
-    in_2 = exchange(after(out_2, in_0))
+    in_2 = exchange(after(out_2, in_0, got_3))
     out_3 = contexts(3, third, 0, got_3, (out_2,), apart=True)
     in_3 = send(out_3)
     result = receive(1, in_1, result, out_3[0])

time: 346 us -> 338 us (0.977)
  waiting for transfers between devices: 140 us -> 132 us
    all_gather x3, waiting for transfers between devices: 20.9 us -> 5.16 us  [local_line(): gathered = lax.all_gather(jnp.stack(group), 'dp', axis_index_groups=along_z)]
    ppermute x7, waiting for transfers between devices: 43.4 us -> 51.6 us  [swap_x(): return lax.ppermute(array, 'dp', [(i, i ^ 1) for i in range(learners)])]
  transfers between devices with their start and end apart: 33 -> 33, of which waited for: 16 -> 16; matrix products, arithmetic and copies ran while one was open for 4% -> 4% of each run, Pallas kernels for 26% -> 27%
where the time goes in v1:
time: 338 us; the launch traced here: 332 us
  waiting for transfers between devices  132 us (39%)
  Pallas kernels  92.3 us (27%)
  starting transfers between devices  46.3 us (14%)
  local copies, waits for them, and re-layouts  35.3 us (10%)
  between operations  13.8 us (4%)
  other arithmetic  11.7 us (3%)
    ppermute x5, waiting for transfers between devices, swap_y(): return lax.ppermute(array, 'tensor', [(i, i ^ 2) for i in range(4)])  65.7 us
    ppermute x7, waiting for transfers between devices, swap_x(): return lax.ppermute(array, 'dp', [(i, i ^ 1) for i in range(learners)])  51.6 us
    pallas_call x8, Pallas kernels, projection(): pl.pallas_call(functools.partial(product_kernel, len(x_parts), ropes, tup...  44.6 us
    unnamed x68, local copies, waits for them, and re-layouts  30.5 us
    pallas_call x4, Pallas kernels, attend(): pl.pallas_call(functools.partial(attend_kernel, columns // HD, window), i...  29.4 us
    all_to_all x3, starting transfers between devices, exchange(): lax.all_to_all(outgoing, 'dp', split_axis=0, concat_axis=0, tiled=True)  16 us
    ppermute x7, starting transfers between devices, send(): incoming.append(lax.ppermute(outgoing[d], 'dp', pairs))  11.2 us
    ppermute x7, starting transfers between devices, swap_x(): return lax.ppermute(array, 'dp', [(i, i ^ 1) for i in range(learners)])  9.54 us
  transfers between devices with their start and end apart: 33, of which 16 were waited for; matrix products, arithmetic and copies ran while one was open for 4% of the time, Pallas kernels for 27%

profile of v1, /device:TPU:0, one launch (start us, length us, event | category | flops | bytes accessed | tf_op | source)
XLA Modules:
  0.0 331.7 jit_solution(8796888070693153033)
XLA Ops:
  11.4 3.1 multiply_reduce_fusion
  20.3 3.5 %multiply_convert_fusion = (bf16[1024,1024]{1,0:T(8,128)(2,1)S(1)}, bf16[1024,1024]{1,0:T(8,128)(2,1)S(1)}) fusion(f32[1024]{0:T(1024)S(1)} %get-tuple-element.83, bf16[1024,2048]{1,0:T(8,128)(2,1)} %param.11, s32[]{:T(128)S(6)} %select_n.29, f32[1024]{0:T(1024)S(1)} %add_rsqrt_fusion, f32[1024]{0:T(1024)S(1)} %get-tuple-element.84, s32[]{:T(128)S(6)} %select_n.27), kind=kLoop, calls=%fused_computation.1 | loop fusion | flops 8388608 | bytes 8400904 | tf_op jit(solution)/shard_map/convert_element_type | solution.py:473
  28.8 20.8 %collective-permute-done.3.refs_2_ = bf16[512,1024]{1,0:T(8,128)(2,1)S(1)} collective-permute-done((bf16[512,1024]{1,0:T(8,128)(2,1)S(1)}, bf16[512,1024]{1,0:T(8,128)(2,1)S(1)}, u32[]{:S(2)}, u32[]{:S(2)}) %collective-permute-start.3) | collective-permute-done | bytes 1048608 | tf_op jit(solution)/shard_map/ppermute | solution.py:444
  53.4 21.3 %collective-permute-done.6.refs_2_ = bf16[512,1024]{1,0:T(8,128)(2,1)} collective-permute-done((bf16[512,1024]{1,0:T(8,128)(2,1)}, bf16[512,1024]{1,0:T(8,128)(2,1)}, u32[]{:S(2)}, u32[]{:S(2)}) %collective-permute-start.6) | collective-permute-done | bytes 1048608 | tf_op jit(solution)/shard_map/ppermute | solution.py:444
  77.3 19.9 %collective-permute-done.7.refs_2_ = bf16[512,1024]{1,0:T(8,128)(2,1)} collective-permute-done((bf16[512,1024]{1,0:T(8,128)(2,1)}, bf16[512,1024]{1,0:T(8,128)(2,1)}, u32[]{:S(2)}, u32[]{:S(2)}) %collective-permute-start.7) | collective-permute-done | bytes 1048608 | tf_op jit(solution)/shard_map/ppermute | solution.py:444
  112.5 7.3 %shard_map.111 = (f32[1024,256]{1,0:T(8,128)S(1)}, bf16[1024,256]{1,0:T(8,128)(2,1)S(1)}) custom-call(s32[4]{0:T(128)S(1)} %pad_add_fusion.which_ref, bf16[4,512,1024]{2,1,0:T(8,128)(2,1)S(1)} %copy-done.14, bf16[4,512,1024]{2,1,0:T(8,128)(2,1)S(1)} %copy-done.18, bf16[4,2,1024,256]{3,2,1,0:T(8,128)(2,1)} %bitcast.36), custom_call_target="tpu_custom_call" | custom-call | flops 4000000000 | bytes 1048576 | tf_op jit(solution)/shard_map/pallas_call | solution.py:257
  126.4 18.7 %collective-permute-done.15.refs_2_ = f32[1024,256]{1,0:T(8,128)S(1)} collective-permute-done((f32[1024,256]{1,0:T(8,128)S(1)}, f32[1024,256]{1,0:T(8,128)S(1)}, u32[]{:S(2)}, u32[]{:S(2)}) %collective-permute-start.15) | collective-permute-done | bytes 1048608 | tf_op jit(solution)/shard_map/ppermute | solution.py:441
  148.9 6.3 %shard_map.113.in_ref = bf16[1024,256]{1,0:T(8,128)(2,1)S(1)} custom-call(s32[4]{0:T(128)S(1)} %pad_add_fusion.which_ref, bf16[4,1024,1024]{2,1,0:T(8,128)(2,1)S(1)} %shard_map.112.refs_0_, bf16[4,2,1024,256]{3,2,1,0:T(8,128)(2,1)} %bitcast.37, f32[1024,256]{1,0:T(8,128)S(1)} %collective-permute-done.15.refs_2_, f32[1,256]{1,0:T(1,128)S(1)} %bitcast.28, ...), custom_call_target="tpu_custom_call" | custom-call | flops 4000000000 | bytes 1048576 | tf_op jit(solution)/shard_map/pallas_call | solution.py:257
  158.3 4.8 %shard_map.114.q_ref = bf16[1024,256]{1,0:T(8,128)(2,1)S(1)} custom-call(s32[4]{0:T(128)S(1)} %pad_add_fusion.which_ref, bf16[4,1024,1024]{2,1,0:T(8,128)(2,1)S(1)} %shard_map.112.refs_0_, bf16[4,2,1024,256]{3,2,1,0:T(8,128)(2,1)} %bitcast.38, bf16[1024,256]{1,0:T(8,128)(2,1)S(1)} %collective-permute-done.16.refs_2_, f32[1,256]{1,0:T(1,128)S(1)} %bitcast.32, ...), custom_call_target="tpu_custom_call" | custom-call | flops 4000000000 | bytes 1048576 | tf_op jit(solution)/shard_map/pallas_call | solution.py:257
  163.1 7.6 %shard_map.116 = bf16[8,256,256]{2,1,0:T(8,128)(2,1)} custom-call(s32[8]{0:T(128)S(1)} %get-tuple-element.50.start_ref, s32[8]{0:T(128)S(1)} %get-tuple-element.65.len_ref, bf16[1024,256]{1,0:T(8,128)(2,1)S(1)} %shard_map.114.q_ref, bf16[8,256,256]{2,1,0:T(8,128)(2,1)S(1)} %shard_map.115.kv_ref), custom_call_target="tpu_custom_call" | custom-call | flops 4000000000 | bytes 1048576 | tf_op jit(solution)/shard_map/pallas_call | solution.py:348
  170.7 6.0 %all-to-all-start = ((bf16[8,256,256]{2,1,0:T(8,128)(2,1)}), bf16[8,256,256]{2,1,0:T(8,128)(2,1)S(1)}, u32[]{:S(2)}, u32[]{:S(2)}) async-start(bf16[8,256,256]{2,1,0:T(8,128)(2,1)} %shard_map.116), calls=%async_computation | async-start | bytes 2097152 | tf_op jit(solution)/shard_map/all_to_all | solution.py:529
  181.1 7.5 %shard_map.117 = (bf16[1024,256]{1,0:T(8,128)(2,1)S(1)}, bf16[1024,256]{1,0:T(8,128)(2,1)S(1)}) custom-call(s32[4]{0:T(128)S(1)} %pad_add_fusion.which_ref, bf16[4,512,1024]{2,1,0:T(8,128)(2,1)S(1)} %copy-done.15, bf16[4,512,1024]{2,1,0:T(8,128)(2,1)S(1)} %copy-done.19, bf16[4,2,1024,256]{3,2,1,0:T(8,128)(2,1)} %bitcast.33), custom_call_target="tpu_custom_call" | custom-call | flops 4000000000 | bytes 1048576 | tf_op jit(solution)/shard_map/pallas_call | solution.py:257
  190.7 13.2 %collective-permute-done.17.refs_2_ = bf16[1024,256]{1,0:T(8,128)(2,1)S(1)} collective-permute-done((bf16[1024,256]{1,0:T(8,128)(2,1)S(1)}, bf16[1024,256]{1,0:T(8,128)(2,1)S(1)}, u32[]{:S(2)}, u32[]{:S(2)}) %collective-permute-start.17) | collective-permute-done | bytes 524320 | tf_op jit(solution)/shard_map/ppermute | solution.py:441
  203.9 3.4 %copy-done.1 = bf16[4,1024,1024]{2,1,0:T(8,128)(2,1)S(1)} copy-done((bf16[4,1024,1024]{2,1,0:T(8,128)(2,1)S(1)}, bf16[4,1024,1024]{2,1,0:T(8,128)(2,1)}, u32[]{:S(2)}) %copy-start.1) | copy-done | bytes 8388632
  207.3 4.8 %shard_map.118.q_ref = bf16[1024,256]{1,0:T(8,128)(2,1)S(1)} custom-call(s32[4]{0:T(128)S(1)} %pad_add_fusion.which_ref, bf16[4,1024,1024]{2,1,0:T(8,128)(2,1)S(1)} %copy-done.1, bf16[4,2,1024,256]{3,2,1,0:T(8,128)(2,1)} %bitcast.34, bf16[1024,256]{1,0:T(8,128)(2,1)S(1)} %collective-permute-done.17.refs_2_, f32[1,256]{1,0:T(1,128)S(1)} %bitcast.31, ...), custom_call_target="tpu_custom_call" | custom-call | flops 4000000000 | bytes 1048576 | tf_op jit(solution)/shard_map/pallas_call | solution.py:257
  212.0 3.5 %collective-permute-done.18.refs_2_ = bf16[1024,256]{1,0:T(8,128)(2,1)S(1)} collective-permute-done((bf16[1024,256]{1,0:T(8,128)(2,1)S(1)}, bf16[1024,256]{1,0:T(8,128)(2,1)S(1)}, u32[]{:S(2)}, u32[]{:S(2)}) %collective-permute-start.18) | collective-permute-done | bytes 524320 | tf_op jit(solution)/shard_map/ppermute | solution.py:441
  215.5 7.6 %shard_map.119 = bf16[8,256,256]{2,1,0:T(8,128)(2,1)} custom-call(s32[8]{0:T(128)S(1)} %get-tuple-element.50.start_ref, s32[8]{0:T(128)S(1)} %get-tuple-element.65.len_ref, bf16[1024,256]{1,0:T(8,128)(2,1)S(1)} %shard_map.118.q_ref, bf16[8,256,256]{2,1,0:T(8,128)(2,1)S(1)} %copy-done.22), custom_call_target="tpu_custom_call" | custom-call | flops 4000000000 | bytes 1048576 | tf_op jit(solution)/shard_map/pallas_call | solution.py:348
  223.1 6.2 %all-to-all-start.2 = ((bf16[8,256,256]{2,1,0:T(8,128)(2,1)}), bf16[8,256,256]{2,1,0:T(8,128)(2,1)S(1)}, u32[]{:S(2)}, u32[]{:S(2)}) async-start(bf16[8,256,256]{2,1,0:T(8,128)(2,1)} %shard_map.119), calls=%async_computation.2 | async-start | bytes 2097152 | tf_op jit(solution)/shard_map/all_to_all | solution.py:529
  229.3 3.4 %copy-done.2 = bf16[4,1024,1024]{2,1,0:T(8,128)(2,1)S(1)} copy-done((bf16[4,1024,1024]{2,1,0:T(8,128)(2,1)S(1)}, bf16[4,1024,1024]{2,1,0:T(8,128)(2,1)}, u32[]{:S(2)}) %copy-start.2) | copy-done | bytes 8388632
  232.7 4.8 %shard_map.120.q_ref = bf16[1024,256]{1,0:T(8,128)(2,1)S(1)} custom-call(s32[4]{0:T(128)S(1)} %pad_add_fusion.which_ref, bf16[4,1024,1024]{2,1,0:T(8,128)(2,1)S(1)} %copy-done.2, bf16[4,2,1024,256]{3,2,1,0:T(8,128)(2,1)} %bitcast.35, bf16[1024,256]{1,0:T(8,128)(2,1)S(1)} %collective-permute-done.18.refs_2_, f32[1,256]{1,0:T(1,128)S(1)} %bitcast.30, ...), custom_call_target="tpu_custom_call" | custom-call | flops 4000000000 | bytes 1048576 | tf_op jit(solution)/shard_map/pallas_call | solution.py:257
  237.5 7.6 %shard_map.121 = bf16[8,256,256]{2,1,0:T(8,128)(2,1)} custom-call(s32[8]{0:T(128)S(1)} %get-tuple-element.50.start_ref, s32[8]{0:T(128)S(1)} %get-tuple-element.65.len_ref, bf16[1024,256]{1,0:T(8,128)(2,1)S(1)} %shard_map.120.q_ref, bf16[8,256,256]{2,1,0:T(8,128)(2,1)S(1)} %copy-done.23), custom_call_target="tpu_custom_call" | custom-call | flops 4000000000 | bytes 1048576 | tf_op jit(solution)/shard_map/pallas_call | solution.py:348
  245.0 5.1 %all-gather.11.cloned.1.call-done = bf16[4096,256]{1,0:T(8,128)(2,1)} async-done(((bf16[1024,256]{1,0:T(8,128)(2,1)}), bf16[4096,256]{1,0:T(8,128)(2,1)}) %all-gather.11.cloned.1.call-update) | async-done | bytes 2097168 | tf_op jit(solution)/shard_map/all_gather | solution.py:458
  254.6 4.4 %shard_map.122 = bf16[1024,256]{1,0:T(8,128)(2,1)S(1)} custom-call(s32[4]{0:T(128)S(1)} %pad_add_fusion.which_ref, bf16[4,512,1024]{2,1,0:T(8,128)(2,1)S(1)} %copy-done.16, bf16[4,512,1024]{2,1,0:T(8,128)(2,1)S(1)} %copy-done.20, bf16[4,1,1024,256]{3,2,1,0:T(8,128)(2,1)} %bitcast.39), custom_call_target="tpu_custom_call" | custom-call | flops 4000000000 | bytes 1048576 | tf_op jit(solution)/shard_map/pallas_call | solution.py:257
  260.3 12.7 %collective-permute-done.19.refs_2_ = bf16[1024,256]{1,0:T(8,128)(2,1)S(1)} collective-permute-done((bf16[1024,256]{1,0:T(8,128)(2,1)S(1)}, bf16[1024,256]{1,0:T(8,128)(2,1)S(1)}, u32[]{:S(2)}, u32[]{:S(2)}) %collective-permute-start.19) | collective-permute-done | bytes 524320 | tf_op jit(solution)/shard_map/ppermute | solution.py:441
  273.7 3.8 %all-to-all-start.1 = ((bf16[8,256,256]{2,1,0:T(8,128)(2,1)}), bf16[8,256,256]{2,1,0:T(8,128)(2,1)S(1)}, u32[]{:S(2)}, u32[]{:S(2)}) async-start(bf16[8,256,256]{2,1,0:T(8,128)(2,1)} %shard_map.121), calls=%async_computation.1 | async-start | bytes 2097152 | tf_op jit(solution)/shard_map/all_to_all | solution.py:529
  279.9 3.4 %copy-done.3 = bf16[4,1024,1024]{2,1,0:T(8,128)(2,1)S(1)} copy-done((bf16[4,1024,1024]{2,1,0:T(8,128)(2,1)S(1)}, bf16[4,1024,1024]{2,1,0:T(8,128)(2,1)}, u32[]{:S(2)}) %copy-start.3) | copy-done | bytes 8388632
  283.3 4.7 %shard_map.123.q_ref = bf16[1024,256]{1,0:T(8,128)(2,1)S(1)} custom-call(s32[4]{0:T(128)S(1)} %pad_add_fusion.which_ref, bf16[4,1024,1024]{2,1,0:T(8,128)(2,1)S(1)} %copy-done.3, bf16[4,1,1024,256]{3,2,1,0:T(8,128)(2,1)} %bitcast.40, bf16[1024,256]{1,0:T(8,128)(2,1)S(1)} %copy-done.8, f32[1,256]{1,0:T(1,128)S(1)} %bitcast.29, f32[1024,128]{1,0:T(8,128)S(1)} %copy-done.6), custom_call_target="tpu_custom_call" | custom-call | flops 4000000000 | bytes 1048576 | tf_op jit(solution)/shard_map/pallas_call | solution.py:257
  288.0 6.6 %shard_map.125 = (bf16[256,256]{1,0:T(8,128)(2,1)S(1)}, bf16[256,256]{1,0:T(8,128)(2,1)S(1)}, bf16[256,256]{1,0:T(8,128)(2,1)S(1)}, bf16[256,256]{1,0:T(8,128)(2...) custom-call(s32[8]{0:T(128)S(1)} %get-tuple-element.67.start_ref, ...), custom_call_target="tpu_custom_call" | custom-call | flops 4000000000 | bytes 1048576 | tf_op jit(solution)/shard_map/pallas_call | solution.py:348
  307.0 3.3 collective-permute-start.25
  313.0 5.9 %collective-permute-done.23.refs_4_ = bf16[256,256]{1,0:T(8,128)(2,1)} collective-permute-done((bf16[256,256]{1,0:T(8,128)(2,1)}, bf16[256,256]{1,0:T(8,128)(2,1)}, u32[]{:S(2)}, u32[]{:S(2)}) %collective-permute-start.23) | collective-permute-done | bytes 131104 | tf_op jit(solution)/shard_map/ppermute | solution.py:525
  318.9 3.1 collective-permute-done.24.refs_5_
  321.9 3.0 shard_map.129
  (153 shorter events, 80.9 us)
Async XLA Ops:
  6.5 101.6 %all-gather.7.cloned.1.call-start = ((), (), s32[]{:S(2)}) async-start(), calls=%async_computation.3 | async-start | bytes 5242880 | tf_op jit(solution)/shard_map/all_gather | solution.py:458
  10.3 166.4 %all-gather.9.cloned.1.call-start = ((), (), s32[]{:S(2)}) async-start(), calls=%async_computation.4 | async-start | bytes 5242880 | tf_op jit(solution)/shard_map/all_gather | solution.py:458
  11.4 238.8 %all-gather.11.cloned.1.call-start = ((), (), s32[]{:S(2)}) async-start(), calls=%async_computation.5 | async-start | bytes 2621440 | tf_op jit(solution)/shard_map/all_gather | solution.py:458
  15.9 4.4 %collective-permute-start.1 = (f32[1024]{0:T(1024)S(1)}, f32[1024]{0:T(1024)S(1)}, u32[]{:S(2)}, u32[]{:S(2)}) collective-permute-start(f32[1024]{0:T(1024)S(1)} %add.48), channel_id=1, source_target_pairs={{0,2},{1,3},{2,0},{3,1},{4,6},{5,7},{6,4},{7,5},{8,10},{9,11},{10,... | collective-permute-start | bytes 12296 | tf_op jit(solution)/shard_map/ppermute | solution.py:444
  25.1 24.5 %collective-permute-start.3 = (bf16[512,1024]{1,0:T(8,128)(2,1)S(1)}, bf16[512,1024]{1,0:T(8,128)(2,1)S(1)}, u32[]{:S(2)}, u32[]{:S(2)}) collective-permute-start(bf16[512,1024]{1,0:T(8,128)(2,1)S(1)} %get-tuple-element.82), channel_id=1, source_target_pairs={{0,2},{1,3},{2,0},{3,1},{4,6},{5,7},{6,4},{7,5},{8,10},{9,11},{10,... | collective-permute-start | bytes 3145736 | tf_op jit(solution)/shard_map/ppermute | solution.py:444
  27.3 24.1 %collective-permute-start.4 = (bf16[512,1024]{1,0:T(8,128)(2,1)S(1)}, bf16[512,1024]{1,0:T(8,128)(2,1)}, u32[]{:S(2)}, u32[]{:S(2)}) collective-permute-start(bf16[512,1024]{1,0:T(8,128)(2,1)S(1)} %get-tuple-element.79), channel_id=1, source_target_pairs={{0,4},{4,0},{8,12},{12,8},{16,20},{20,16},{24,28},{28,24},{1,5},{5... | collective-permute-start | bytes 3145736 | tf_op jit(solution)/shard_map/ppermute | solution.py:441
  51.4 23.3 %collective-permute-start.6 = (bf16[512,1024]{1,0:T(8,128)(2,1)}, bf16[512,1024]{1,0:T(8,128)(2,1)}, u32[]{:S(2)}, u32[]{:S(2)}) collective-permute-start(bf16[512,1024]{1,0:T(8,128)(2,1)} %collective-permute-done.4.refs_0_), channel_id=1, source_target_pairs={{0,2},{1,3},{2,0},{3,1},{4,6},{5,7},{6,4},{7,5},{8,10},{9,11},{10,... | collective-permute-start | bytes 3145736 | tf_op jit(solution)/shard_map/ppermute | solution.py:444
  51.7 23.1 %collective-permute-start.5 = (bf16[512,1024]{1,0:T(8,128)(2,1)S(1)}, bf16[512,1024]{1,0:T(8,128)(2,1)}, u32[]{:S(2)}, u32[]{:S(2)}) collective-permute-start(bf16[512,1024]{1,0:T(8,128)(2,1)S(1)} %get-tuple-element.35), channel_id=1, source_target_pairs={{0,4},{4,0},{8,12},{12,8},{16,20},{20,16},{24,28},{28,24},{1,5},{5... | collective-permute-start | bytes 3145736 | tf_op jit(solution)/shard_map/ppermute | solution.py:441
  74.8 22.4 %collective-permute-start.7 = (bf16[512,1024]{1,0:T(8,128)(2,1)}, bf16[512,1024]{1,0:T(8,128)(2,1)}, u32[]{:S(2)}, u32[]{:S(2)}) collective-permute-start(bf16[512,1024]{1,0:T(8,128)(2,1)} %collective-permute-done.5.refs_0_), channel_id=1, source_target_pairs={{0,2},{1,3},{2,0},{3,1},{4,6},{5,7},{6,4},{7,5},{8,10},{9,11},{10,... | collective-permute-start | bytes 3145736 | tf_op jit(solution)/shard_map/ppermute | solution.py:444
  76.2 22.0 %collective-permute-start.10 = (bf16[512,1024]{1,0:T(8,128)(2,1)}, bf16[512,1024]{1,0:T(8,128)(2,1)}, u32[]{:S(2)}, u32[]{:S(2)}) collective-permute-start(bf16[512,1024]{1,0:T(8,128)(2,1)} %collective-permute-done.4.refs_0_), channel_id=1, source_target_pairs={{0,1},{1,0},{2,3},{3,2},{4,5},{5,4},{6,7},{7,6},{8,9},{9,8},{10,11... | collective-permute-start | bytes 3145736 | tf_op jit(solution)/shard_map/ppermute | solution.py:447
  76.2 22.1 %collective-permute-start.11 = (bf16[512,1024]{1,0:T(8,128)(2,1)}, bf16[512,1024]{1,0:T(8,128)(2,1)}, u32[]{:S(2)}, u32[]{:S(2)}) collective-permute-start(bf16[512,1024]{1,0:T(8,128)(2,1)} %collective-permute-done.6.refs_2_), channel_id=1, source_target_pairs={{0,1},{1,0},{2,3},{3,2},{4,5},{5,4},{6,7},{7,6},{8,9},{9,8},{10,11... | collective-permute-start | bytes 3145736 | tf_op jit(solution)/shard_map/ppermute | solution.py:447
  77.3 26.9 %collective-permute-start.12 = (bf16[512,1024]{1,0:T(8,128)(2,1)}, bf16[512,1024]{1,0:T(8,128)(2,1)S(1)}, u32[]{:S(2)}, u32[]{:S(2)}) collective-permute-start(bf16[512,1024]{1,0:T(8,128)(2,1)} %collective-permute-done.5.refs_0_), channel_id=1, source_target_pairs={{0,1},{1,0},{2,3},{3,2},{4,5},{5,4},{6,7},{7,6},{8,9},{9,8},{10,11... | collective-permute-start | bytes 3145736 | tf_op jit(solution)/shard_map/ppermute | solution.py:447
  97.2 6.9 %collective-permute-start.13 = (bf16[512,1024]{1,0:T(8,128)(2,1)}, bf16[512,1024]{1,0:T(8,128)(2,1)S(1)}, u32[]{:S(2)}, u32[]{:S(2)}) collective-permute-start(bf16[512,1024]{1,0:T(8,128)(2,1)} %collective-permute-done.7.refs_2_), channel_id=1, source_target_pairs={{0,1},{1,0},{2,3},{3,2},{4,5},{5,4},{6,7},{7,6},{8,9},{9,8},{10,11... | collective-permute-start | bytes 3145736 | tf_op jit(solution)/shard_map/ppermute | solution.py:447
  97.6 48.8 %collective-permute-start.2 = (bf16[1024,1024]{1,0:T(8,128)(2,1)S(1)}, bf16[1024,1024]{1,0:T(8,128)(2,1)}, u32[]{:S(2)}, u32[]{:S(2)}) collective-permute-start(bf16[1024,1024]{1,0:T(8,128)(2,1)S(1)} %get-tuple-element.74.refs_0_), channel_id=1, source_target_pairs={{0,1},{1,0},{2,3},{3,2},{4,5},{5,4},{6,7},{7,6},{8,9},{9,8},{10,11... | collective-permute-start | bytes 6291464 | tf_op jit(solution)/shard_map/ppermute | solution.py:447
  98.2 48.3 %collective-permute-start.9 = (bf16[512,1024]{1,0:T(8,128)(2,1)S(1)}, bf16[512,1024]{1,0:T(8,128)(2,1)}, u32[]{:S(2)}, u32[]{:S(2)}) collective-permute-start(bf16[512,1024]{1,0:T(8,128)(2,1)S(1)} %collective-permute-done.3.refs_2_), channel_id=1, source_target_pairs={{0,1},{1,0},{2,3},{3,2},{4,5},{5,4},{6,7},{7,6},{8,9},{9,8},{10,11... | collective-permute-start | bytes 3145736 | tf_op jit(solution)/shard_map/ppermute | solution.py:447
  98.3 25.8 %collective-permute-start.8 = (bf16[512,1024]{1,0:T(8,128)(2,1)}, bf16[512,1024]{1,0:T(8,128)(2,1)}, u32[]{:S(2)}, u32[]{:S(2)}) collective-permute-start(bf16[512,1024]{1,0:T(8,128)(2,1)} %get-tuple-element.38), channel_id=1, source_target_pairs={{0,2},{1,3},{2,0},{3,1},{4,6},{5,7},{6,4},{7,5},{8,10},{9,11},{10,... | collective-permute-start | bytes 3145736 | tf_op jit(solution)/shard_map/ppermute | solution.py:444
  119.8 25.3 %collective-permute-start.15 = (f32[1024,256]{1,0:T(8,128)S(1)}, f32[1024,256]{1,0:T(8,128)S(1)}, u32[]{:S(2)}, u32[]{:S(2)}) collective-permute-start(f32[1024,256]{1,0:T(8,128)S(1)} %get-tuple-element.41), channel_id=1, source_target_pairs={{0,4},{4,0},{8,12},{12,8},{16,20},{20,16},{24,28},{28,24},{1,5},{5... | collective-permute-start | bytes 3145736 | tf_op jit(solution)/shard_map/ppermute | solution.py:441
  124.1 22.4 %collective-permute-start.14 = (bf16[512,1024]{1,0:T(8,128)(2,1)}, bf16[512,1024]{1,0:T(8,128)(2,1)S(1)}, u32[]{:S(2)}, u32[]{:S(2)}) collective-permute-start(bf16[512,1024]{1,0:T(8,128)(2,1)} %collective-permute-done.8.refs_3_), channel_id=1, source_target_pairs={{0,1},{1,0},{2,3},{3,2},{4,5},{5,4},{6,7},{7,6},{8,9},{9,8},{10,11... | collective-permute-start | bytes 3145736 | tf_op jit(solution)/shard_map/ppermute | solution.py:447
  145.1 13.3 %collective-permute-start.16 = (bf16[1024,256]{1,0:T(8,128)(2,1)S(1)}, bf16[1024,256]{1,0:T(8,128)(2,1)S(1)}, u32[]{:S(2)}, u32[]{:S(2)}) collective-permute-start(bf16[1024,256]{1,0:T(8,128)(2,1)S(1)} %get-tuple-element.45), channel_id=1, source_target_pairs={{0,4},{4,0},{8,12},{12,8},{16,20},{20,16},{24,28},{28,24},{1,5},{5... | collective-permute-start | bytes 1572872 | tf_op jit(solution)/shard_map/ppermute | solution.py:441
  170.7 52.4 %all-to-all-start = ((bf16[8,256,256]{2,1,0:T(8,128)(2,1)}), bf16[8,256,256]{2,1,0:T(8,128)(2,1)S(1)}, u32[]{:S(2)}, u32[]{:S(2)}) async-start(bf16[8,256,256]{2,1,0:T(8,128)(2,1)} %shard_map.116), calls=%async_computation | async-start | bytes 2097152 | tf_op jit(solution)/shard_map/all_to_all | solution.py:529
  188.6 15.3 %collective-permute-start.17 = (bf16[1024,256]{1,0:T(8,128)(2,1)S(1)}, bf16[1024,256]{1,0:T(8,128)(2,1)S(1)}, u32[]{:S(2)}, u32[]{:S(2)}) collective-permute-start(bf16[1024,256]{1,0:T(8,128)(2,1)S(1)} %get-tuple-element.48), channel_id=1, source_target_pairs={{0,4},{4,0},{8,12},{12,8},{16,20},{20,16},{24,28},{28,24},{1,5},{5... | collective-permute-start | bytes 1572872 | tf_op jit(solution)/shard_map/ppermute | solution.py:441
  203.9 11.6 %collective-permute-start.18 = (bf16[1024,256]{1,0:T(8,128)(2,1)S(1)}, bf16[1024,256]{1,0:T(8,128)(2,1)S(1)}, u32[]{:S(2)}, u32[]{:S(2)}) collective-permute-start(bf16[1024,256]{1,0:T(8,128)(2,1)S(1)} %get-tuple-element.49), channel_id=1, source_target_pairs={{0,4},{4,0},{8,12},{12,8},{16,20},{20,16},{24,28},{28,24},{1,5},{5... | collective-permute-start | bytes 1572872 | tf_op jit(solution)/shard_map/ppermute | solution.py:441
  223.1 50.6 %all-to-all-start.2 = ((bf16[8,256,256]{2,1,0:T(8,128)(2,1)}), bf16[8,256,256]{2,1,0:T(8,128)(2,1)S(1)}, u32[]{:S(2)}, u32[]{:S(2)}) async-start(bf16[8,256,256]{2,1,0:T(8,128)(2,1)} %shard_map.119), calls=%async_computation.2 | async-start | bytes 2097152 | tf_op jit(solution)/shard_map/all_to_all | solution.py:529
  259.0 14.0 %collective-permute-start.19 = (bf16[1024,256]{1,0:T(8,128)(2,1)S(1)}, bf16[1024,256]{1,0:T(8,128)(2,1)S(1)}, u32[]{:S(2)}, u32[]{:S(2)}) collective-permute-start(bf16[1024,256]{1,0:T(8,128)(2,1)S(1)} %shard_map.122), channel_id=1, source_target_pairs={{0,4},{4,0},{8,12},{12,8},{16,20},{20,16},{24,28},{28,24},{1,5},{5... | collective-permute-start | bytes 1572872 | tf_op jit(solution)/shard_map/ppermute | solution.py:441
  273.7 37.3 %all-to-all-start.1 = ((bf16[8,256,256]{2,1,0:T(8,128)(2,1)}), bf16[8,256,256]{2,1,0:T(8,128)(2,1)S(1)}, u32[]{:S(2)}, u32[]{:S(2)}) async-start(bf16[8,256,256]{2,1,0:T(8,128)(2,1)} %shard_map.121), calls=%async_computation.1 | async-start | bytes 2097152 | tf_op jit(solution)/shard_map/all_to_all | solution.py:529
  295.3 11.7 %collective-permute-start.20 = (bf16[256,256]{1,0:T(8,128)(2,1)S(1)}, bf16[256,256]{1,0:T(8,128)(2,1)S(1)}, u32[]{:S(2)}, u32[]{:S(2)}) collective-permute-start(bf16[256,256]{1,0:T(8,128)(2,1)S(1)} %get-tuple-element.55), channel_id=1, source_target_pairs={{0,4},{4,0},{8,12},{12,8},{16,20},{20,16},{24,28},{28,24},{1,5},{5... | collective-permute-start | bytes 393224 | tf_op jit(solution)/shard_map/ppermute | solution.py:525
  297.3 13.0 %collective-permute-start.21 = (bf16[256,256]{1,0:T(8,128)(2,1)S(1)}, bf16[256,256]{1,0:T(8,128)(2,1)S(1)}, u32[]{:S(2)}, u32[]{:S(2)}) collective-permute-start(bf16[256,256]{1,0:T(8,128)(2,1)S(1)} %get-tuple-element.56), channel_id=1, source_target_pairs={{0,8},{4,12},{8,0},{12,4},{16,24},{20,28},{24,16},{28,20},{1,9},{5... | collective-permute-start | bytes 393224 | tf_op jit(solution)/shard_map/ppermute | solution.py:525
  298.8 14.2 %collective-permute-start.22 = (bf16[256,256]{1,0:T(8,128)(2,1)}, bf16[256,256]{1,0:T(8,128)(2,1)}, u32[]{:S(2)}, u32[]{:S(2)}) collective-permute-start(bf16[256,256]{1,0:T(8,128)(2,1)} %get-tuple-element.57), channel_id=1, source_target_pairs={{0,12},{4,8},{8,4},{12,0},{16,28},{20,24},{24,20},{28,16},{1,13},{... | collective-permute-start | bytes 393224 | tf_op jit(solution)/shard_map/ppermute | solution.py:525
  298.8 20.0 %collective-permute-start.23 = (bf16[256,256]{1,0:T(8,128)(2,1)}, bf16[256,256]{1,0:T(8,128)(2,1)}, u32[]{:S(2)}, u32[]{:S(2)}) collective-permute-start(bf16[256,256]{1,0:T(8,128)(2,1)} %get-tuple-element.58), channel_id=1, source_target_pairs={{0,16},{4,20},{8,24},{12,28},{16,0},{20,4},{24,8},{28,12},{1,17},{... | collective-permute-start | bytes 393224 | tf_op jit(solution)/shard_map/ppermute | solution.py:525
  301.7 20.2 %collective-permute-start.24 = (bf16[256,256]{1,0:T(8,128)(2,1)}, bf16[256,256]{1,0:T(8,128)(2,1)}, u32[]{:S(2)}, u32[]{:S(2)}) collective-permute-start(bf16[256,256]{1,0:T(8,128)(2,1)} %get-tuple-element.59), channel_id=1, source_target_pairs={{0,20},{4,16},{8,28},{12,24},{16,4},{20,0},{24,12},{28,8},{1,21},{... | collective-permute-start | bytes 393224 | tf_op jit(solution)/shard_map/ppermute | solution.py:525
  307.0 14.9 %collective-permute-start.25 = (bf16[256,256]{1,0:T(8,128)(2,1)}, bf16[256,256]{1,0:T(8,128)(2,1)S(1)}, u32[]{:S(2)}, u32[]{:S(2)}) collective-permute-start(bf16[256,256]{1,0:T(8,128)(2,1)} %get-tuple-element.60), channel_id=1, source_target_pairs={{0,24},{4,28},{8,16},{12,20},{16,8},{20,12},{24,0},{28,4},{1,25},{... | collective-permute-start | bytes 393224 | tf_op jit(solution)/shard_map/ppermute | solution.py:525
  311.0 11.0 %collective-permute-start.26 = (bf16[256,256]{1,0:T(8,128)(2,1)S(1)}, bf16[256,256]{1,0:T(8,128)(2,1)S(1)}, u32[]{:S(2)}, u32[]{:S(2)}) collective-permute-start(bf16[256,256]{1,0:T(8,128)(2,1)S(1)} %get-tuple-element.61), channel_id=1, source_target_pairs={{0,28},{4,24},{8,20},{12,16},{16,12},{20,8},{24,4},{28,0},{1,29},{... | collective-permute-start | bytes 393224 | tf_op jit(solution)/shard_map/ppermute | solution.py:525
  (35 other events, 467.2 us)
Sparse Core Ops, SparseCore 0:
  10.4 83.4 all-gather.6
  95.4 79.2 all-gather.8
  176.3 73.7 all-gather.10

commit v2 on v1

--- a/solution.py
+++ b/solution.py
@@ -539,13 +539,12 @@
     def partial(group, chunks, outs, *others):
         return projection(after(which, *others), near_x, group, chunks, outs)
 
-    def contexts(c, group, chunk, got, others, attend_after=(), apart=False):
+    def contexts(c, group, chunk, got, others, attend_after=()):
         ending = ((True, True), got, biases[c], angles)
         (rot,) = projection(after(which, *others), own_x, group, (chunk,), whole, ending)
-        send_start, send_length = send_to if apart else send_all
+        send_start, send_length = send_all
         start_at = after(send_start, *attend_after)
-        slots = kv_slots_to if apart else kv_slots
-        return attend(start_at, send_length, rot, slots, window, apart)
+        return attend(start_at, send_length, rot, kv_slots, window, False)
 
     outs = [(0, wide, jnp.float32), (wide, 2 * wide, jnp.bfloat16)]
     part_kv, part_0 = partial(first, (0, 1), outs)
@@ -569,8 +568,10 @@
     (part_3,) = partial(third, (0,), whole, out_2)
     got_3 = swap_x(part_3)
     result = receive(0, in_0, None, part_3)
-    in_2 = exchange(after(out_2, in_0, got_3))
-    out_3 = contexts(3, third, 0, got_3, (out_2,), apart=True)
+    ending = ((True, True), got_3, biases[3], angles)
+    (rot_3,) = projection(after(which, out_2), own_x, third, (0,), whole, ending)
+    in_2 = exchange(after(out_2, in_0, rot_3))
+    out_3 = attend(*send_to, rot_3, kv_slots_to, window, True)
     in_3 = send(out_3)
     result = receive(1, in_1, result, out_3[0])
     result = receive(2, in_2, result, out_3[0])

time: 338 us -> 346 us (1.024)
  waiting for transfers between devices: 132 us -> 139 us
    all_to_all x3, waiting for transfers between devices: 0.01 us -> 12 us  [exchange(): lax.all_to_all(outgoing, 'dp', split_axis=0, concat_axis=0, tiled=True)]
    ppermute x7, waiting for transfers between devices: 8.93 us -> 3.98 us  [send(): incoming.append(lax.ppermute(outgoing[d], 'dp', pairs))]
    unnamed x68 -> x66, local copies, waits for them, and re-layouts: 30.5 us -> 30.5 us
  transfers between devices with their start and end apart: 33 -> 33, of which waited for: 16 -> 17; matrix products, arithmetic and copies ran while one was open for 4% -> 4% of each run, Pallas kernels for 27% -> 26%
where the time goes in v2:
time: 346 us; the launch traced here: 340 us
  waiting for transfers between devices  139 us (40%)
  Pallas kernels  92.3 us (27%)
  starting transfers between devices  47.3 us (14%)
  local copies, waits for them, and re-layouts  35.3 us (10%)
  between operations  13.8 us (4%)
  other arithmetic  11.7 us (3%)
    ppermute x5, waiting for transfers between devices, swap_y(): return lax.ppermute(array, 'tensor', [(i, i ^ 2) for i in range(4)])  65.7 us
    ppermute x7, waiting for transfers between devices, swap_x(): return lax.ppermute(array, 'dp', [(i, i ^ 1) for i in range(learners)])  51.6 us
    pallas_call x8, Pallas kernels, projection(): pl.pallas_call(functools.partial(product_kernel, len(x_parts), ropes, tup...  44.6 us
    unnamed x66, local copies, waits for them, and re-layouts  30.5 us
    pallas_call x4, Pallas kernels, attend(): pl.pallas_call(functools.partial(attend_kernel, columns // HD, window), i...  29.4 us
    all_to_all x3, starting transfers between devices, exchange(): lax.all_to_all(outgoing, 'dp', split_axis=0, concat_axis=0, tiled=True)  16 us
    ppermute x7, starting transfers between devices, send(): incoming.append(lax.ppermute(outgoing[d], 'dp', pairs))  12.1 us
    all_to_all x3, waiting for transfers between devices, exchange(): lax.all_to_all(outgoing, 'dp', split_axis=0, concat_axis=0, tiled=True)  12 us
  transfers between devices with their start and end apart: 33, of which 17 were waited for; matrix products, arithmetic and copies ran while one was open for 4% of the time, Pallas kernels for 26%

profile of v2, /device:TPU:0, one launch (start us, length us, event | category | flops | bytes accessed | tf_op | source)
XLA Modules:
  0.0 339.7 jit_solution(13389799752403505968)
XLA Ops:
  11.4 3.1 multiply_reduce_fusion
  20.3 3.6 %multiply_convert_fusion = (bf16[1024,1024]{1,0:T(8,128)(2,1)S(1)}, bf16[1024,1024]{1,0:T(8,128)(2,1)S(1)}) fusion(f32[1024]{0:T(1024)S(1)} %get-tuple-element.83, bf16[1024,2048]{1,0:T(8,128)(2,1)} %param.11, s32[]{:T(128)S(6)} %select_n.29, f32[1024]{0:T(1024)S(1)} %add_rsqrt_fusion, f32[1024]{0:T(1024)S(1)} %get-tuple-element.84, s32[]{:T(128)S(6)} %select_n.27), kind=kLoop, calls=%fused_computation.1 | loop fusion | flops 8388608 | bytes 8400904 | tf_op jit(solution)/shard_map/convert_element_type | solution.py:473
  28.8 20.8 %collective-permute-done.3.refs_2_ = bf16[512,1024]{1,0:T(8,128)(2,1)S(1)} collective-permute-done((bf16[512,1024]{1,0:T(8,128)(2,1)S(1)}, bf16[512,1024]{1,0:T(8,128)(2,1)S(1)}, u32[]{:S(2)}, u32[]{:S(2)}) %collective-permute-start.3) | collective-permute-done | bytes 1048608 | tf_op jit(solution)/shard_map/ppermute | solution.py:444
  53.3 21.3 %collective-permute-done.6.refs_2_ = bf16[512,1024]{1,0:T(8,128)(2,1)} collective-permute-done((bf16[512,1024]{1,0:T(8,128)(2,1)}, bf16[512,1024]{1,0:T(8,128)(2,1)}, u32[]{:S(2)}, u32[]{:S(2)}) %collective-permute-start.6) | collective-permute-done | bytes 1048608 | tf_op jit(solution)/shard_map/ppermute | solution.py:444
  77.3 19.9 %collective-permute-done.7.refs_2_ = bf16[512,1024]{1,0:T(8,128)(2,1)} collective-permute-done((bf16[512,1024]{1,0:T(8,128)(2,1)}, bf16[512,1024]{1,0:T(8,128)(2,1)}, u32[]{:S(2)}, u32[]{:S(2)}) %collective-permute-start.7) | collective-permute-done | bytes 1048608 | tf_op jit(solution)/shard_map/ppermute | solution.py:444
  112.5 7.3 %shard_map.111 = (f32[1024,256]{1,0:T(8,128)S(1)}, bf16[1024,256]{1,0:T(8,128)(2,1)S(1)}) custom-call(s32[4]{0:T(128)S(1)} %pad_add_fusion.which_ref, bf16[4,512,1024]{2,1,0:T(8,128)(2,1)S(1)} %copy-done.11, bf16[4,512,1024]{2,1,0:T(8,128)(2,1)S(1)} %copy-done.15, bf16[4,2,1024,256]{3,2,1,0:T(8,128)(2,1)} %bitcast.36), custom_call_target="tpu_custom_call" | custom-call | flops 4000000000 | bytes 1048576 | tf_op jit(solution)/shard_map/pallas_call | solution.py:257
  126.3 18.7 %collective-permute-done.15.refs_2_ = f32[1024,256]{1,0:T(8,128)S(1)} collective-permute-done((f32[1024,256]{1,0:T(8,128)S(1)}, f32[1024,256]{1,0:T(8,128)S(1)}, u32[]{:S(2)}, u32[]{:S(2)}) %collective-permute-start.15) | collective-permute-done | bytes 1048608 | tf_op jit(solution)/shard_map/ppermute | solution.py:441
  148.9 6.3 %shard_map.113.in_ref = bf16[1024,256]{1,0:T(8,128)(2,1)S(1)} custom-call(s32[4]{0:T(128)S(1)} %pad_add_fusion.which_ref, bf16[4,1024,1024]{2,1,0:T(8,128)(2,1)S(1)} %shard_map.112.refs_0_, bf16[4,2,1024,256]{3,2,1,0:T(8,128)(2,1)} %bitcast.37, f32[1024,256]{1,0:T(8,128)S(1)} %collective-permute-done.15.refs_2_, f32[1,256]{1,0:T(1,128)S(1)} %bitcast.28, ...), custom_call_target="tpu_custom_call" | custom-call | flops 4000000000 | bytes 1048576 | tf_op jit(solution)/shard_map/pallas_call | solution.py:257
  158.3 4.8 %shard_map.114.q_ref = bf16[1024,256]{1,0:T(8,128)(2,1)S(1)} custom-call(s32[4]{0:T(128)S(1)} %pad_add_fusion.which_ref, bf16[4,1024,1024]{2,1,0:T(8,128)(2,1)S(1)} %shard_map.112.refs_0_, bf16[4,2,1024,256]{3,2,1,0:T(8,128)(2,1)} %bitcast.38, bf16[1024,256]{1,0:T(8,128)(2,1)S(1)} %collective-permute-done.16.refs_2_, f32[1,256]{1,0:T(1,128)S(1)} %bitcast.32, ...), custom_call_target="tpu_custom_call" | custom-call | flops 4000000000 | bytes 1048576 | tf_op jit(solution)/shard_map/pallas_call | solution.py:257
  163.1 7.6 %shard_map.116 = bf16[8,256,256]{2,1,0:T(8,128)(2,1)} custom-call(s32[8]{0:T(128)S(1)} %get-tuple-element.50.start_ref, s32[8]{0:T(128)S(1)} %get-tuple-element.65.len_ref, bf16[1024,256]{1,0:T(8,128)(2,1)S(1)} %shard_map.114.q_ref, bf16[8,256,256]{2,1,0:T(8,128)(2,1)S(1)} %shard_map.115.kv_ref), custom_call_target="tpu_custom_call" | custom-call | flops 4000000000 | bytes 1048576 | tf_op jit(solution)/shard_map/pallas_call | solution.py:348
  170.7 6.0 %all-to-all-start = ((bf16[8,256,256]{2,1,0:T(8,128)(2,1)}), bf16[8,256,256]{2,1,0:T(8,128)(2,1)S(1)}, u32[]{:S(2)}, u32[]{:S(2)}) async-start(bf16[8,256,256]{2,1,0:T(8,128)(2,1)} %shard_map.116), calls=%async_computation | async-start | bytes 2097152 | tf_op jit(solution)/shard_map/all_to_all | solution.py:529
  181.1 7.5 %shard_map.117 = (bf16[1024,256]{1,0:T(8,128)(2,1)S(1)}, bf16[1024,256]{1,0:T(8,128)(2,1)S(1)}) custom-call(s32[4]{0:T(128)S(1)} %pad_add_fusion.which_ref, bf16[4,512,1024]{2,1,0:T(8,128)(2,1)S(1)} %copy-done.12, bf16[4,512,1024]{2,1,0:T(8,128)(2,1)S(1)} %copy-done.16, bf16[4,2,1024,256]{3,2,1,0:T(8,128)(2,1)} %bitcast.33), custom_call_target="tpu_custom_call" | custom-call | flops 4000000000 | bytes 1048576 | tf_op jit(solution)/shard_map/pallas_call | solution.py:257
  190.7 13.2 %collective-permute-done.17.refs_2_ = bf16[1024,256]{1,0:T(8,128)(2,1)S(1)} collective-permute-done((bf16[1024,256]{1,0:T(8,128)(2,1)S(1)}, bf16[1024,256]{1,0:T(8,128)(2,1)S(1)}, u32[]{:S(2)}, u32[]{:S(2)}) %collective-permute-start.17) | collective-permute-done | bytes 524320 | tf_op jit(solution)/shard_map/ppermute | solution.py:441
  203.9 3.4 copy-done.1
  207.3 4.8 %shard_map.118.q_ref = bf16[1024,256]{1,0:T(8,128)(2,1)S(1)} custom-call(s32[4]{0:T(128)S(1)} %pad_add_fusion.which_ref, bf16[4,1024,1024]{2,1,0:T(8,128)(2,1)S(1)} %copy-done.1, bf16[4,2,1024,256]{3,2,1,0:T(8,128)(2,1)} %bitcast.34, bf16[1024,256]{1,0:T(8,128)(2,1)S(1)} %collective-permute-done.17.refs_2_, f32[1,256]{1,0:T(1,128)S(1)} %bitcast.31, ...), custom_call_target="tpu_custom_call" | custom-call | flops 4000000000 | bytes 1048576 | tf_op jit(solution)/shard_map/pallas_call | solution.py:257
  212.0 3.4 %collective-permute-done.18.refs_2_ = bf16[1024,256]{1,0:T(8,128)(2,1)S(1)} collective-permute-done((bf16[1024,256]{1,0:T(8,128)(2,1)S(1)}, bf16[1024,256]{1,0:T(8,128)(2,1)S(1)}, u32[]{:S(2)}, u32[]{:S(2)}) %collective-permute-start.18) | collective-permute-done | bytes 524320 | tf_op jit(solution)/shard_map/ppermute | solution.py:441
  215.5 7.6 %shard_map.119 = bf16[8,256,256]{2,1,0:T(8,128)(2,1)} custom-call(s32[8]{0:T(128)S(1)} %get-tuple-element.50.start_ref, s32[8]{0:T(128)S(1)} %get-tuple-element.65.len_ref, bf16[1024,256]{1,0:T(8,128)(2,1)S(1)} %shard_map.118.q_ref, bf16[8,256,256]{2,1,0:T(8,128)(2,1)S(1)} %copy-done.21), custom_call_target="tpu_custom_call" | custom-call | flops 4000000000 | bytes 1048576 | tf_op jit(solution)/shard_map/pallas_call | solution.py:348
  223.1 6.2 %all-to-all-start.2 = ((bf16[8,256,256]{2,1,0:T(8,128)(2,1)}), bf16[8,256,256]{2,1,0:T(8,128)(2,1)S(1)}, u32[]{:S(2)}, u32[]{:S(2)}) async-start(bf16[8,256,256]{2,1,0:T(8,128)(2,1)} %shard_map.119), calls=%async_computation.2 | async-start | bytes 2097152 | tf_op jit(solution)/shard_map/all_to_all | solution.py:529
  229.3 3.4 copy-done.2
  232.7 4.8 %shard_map.120.q_ref = bf16[1024,256]{1,0:T(8,128)(2,1)S(1)} custom-call(s32[4]{0:T(128)S(1)} %pad_add_fusion.which_ref, bf16[4,1024,1024]{2,1,0:T(8,128)(2,1)S(1)} %copy-done.2, bf16[4,2,1024,256]{3,2,1,0:T(8,128)(2,1)} %bitcast.35, bf16[1024,256]{1,0:T(8,128)(2,1)S(1)} %collective-permute-done.18.refs_2_, f32[1,256]{1,0:T(1,128)S(1)} %bitcast.30, ...), custom_call_target="tpu_custom_call" | custom-call | flops 4000000000 | bytes 1048576 | tf_op jit(solution)/shard_map/pallas_call | solution.py:257
  237.5 7.6 %shard_map.121 = bf16[8,256,256]{2,1,0:T(8,128)(2,1)} custom-call(s32[8]{0:T(128)S(1)} %get-tuple-element.50.start_ref, s32[8]{0:T(128)S(1)} %get-tuple-element.65.len_ref, bf16[1024,256]{1,0:T(8,128)(2,1)S(1)} %shard_map.120.q_ref, bf16[8,256,256]{2,1,0:T(8,128)(2,1)S(1)} %copy-done.22), custom_call_target="tpu_custom_call" | custom-call | flops 4000000000 | bytes 1048576 | tf_op jit(solution)/shard_map/pallas_call | solution.py:348
  245.0 5.1 %all-gather.11.cloned.1.call-done = bf16[4096,256]{1,0:T(8,128)(2,1)} async-done(((bf16[1024,256]{1,0:T(8,128)(2,1)}), bf16[4096,256]{1,0:T(8,128)(2,1)}) %all-gather.11.cloned.1.call-update) | async-done | bytes 2097168 | tf_op jit(solution)/shard_map/all_gather | solution.py:458
  254.5 4.4 %shard_map.122 = bf16[1024,256]{1,0:T(8,128)(2,1)S(1)} custom-call(s32[4]{0:T(128)S(1)} %pad_add_fusion.which_ref, bf16[4,512,1024]{2,1,0:T(8,128)(2,1)S(1)} %copy-done.13, bf16[4,512,1024]{2,1,0:T(8,128)(2,1)S(1)} %copy-done.17, bf16[4,1,1024,256]{3,2,1,0:T(8,128)(2,1)} %bitcast.39), custom_call_target="tpu_custom_call" | custom-call | flops 4000000000 | bytes 1048576 | tf_op jit(solution)/shard_map/pallas_call | solution.py:257
  260.3 12.6 %collective-permute-done.19.refs_2_ = bf16[1024,256]{1,0:T(8,128)(2,1)S(1)} collective-permute-done((bf16[1024,256]{1,0:T(8,128)(2,1)S(1)}, bf16[1024,256]{1,0:T(8,128)(2,1)S(1)}, u32[]{:S(2)}, u32[]{:S(2)}) %collective-permute-start.19) | collective-permute-done | bytes 524320 | tf_op jit(solution)/shard_map/ppermute | solution.py:441
  272.9 3.4 copy-done.3
  276.3 4.8 %shard_map.123.q_ref = bf16[1024,256]{1,0:T(8,128)(2,1)S(1)} custom-call(s32[4]{0:T(128)S(1)} %pad_add_fusion.which_ref, bf16[4,1024,1024]{2,1,0:T(8,128)(2,1)S(1)} %copy-done.3, bf16[4,1,1024,256]{3,2,1,0:T(8,128)(2,1)} %bitcast.40, bf16[1024,256]{1,0:T(8,128)(2,1)S(1)} %collective-permute-done.19.refs_2_, f32[1,256]{1,0:T(1,128)S(1)} %bitcast.29, ...), custom_call_target="tpu_custom_call" | custom-call | flops 4000000000 | bytes 1048576 | tf_op jit(solution)/shard_map/pallas_call | solution.py:257
  281.9 3.8 %all-to-all-start.1 = ((bf16[8,256,256]{2,1,0:T(8,128)(2,1)}), bf16[8,256,256]{2,1,0:T(8,128)(2,1)S(1)}, u32[]{:S(2)}, u32[]{:S(2)}) async-start(bf16[8,256,256]{2,1,0:T(8,128)(2,1)} %shard_map.121), calls=%async_computation.1 | async-start | bytes 2097152 | tf_op jit(solution)/shard_map/all_to_all | solution.py:529
  288.0 6.6 %shard_map.125 = (bf16[256,256]{1,0:T(8,128)(2,1)S(1)}, bf16[256,256]{1,0:T(8,128)(2,1)S(1)}, bf16[256,256]{1,0:T(8,128)(2,1)S(1)}, bf16[256,256]{1,0:T(8,128)(2...) custom-call(s32[8]{0:T(128)S(1)} %get-tuple-element.67.start_ref, ...), custom_call_target="tpu_custom_call" | custom-call | flops 4000000000 | bytes 1048576 | tf_op jit(solution)/shard_map/pallas_call | solution.py:348
  307.0 3.3 collective-permute-start.25
  312.0 12.0 %all-to-all-done.1.refs_0_.refs_1_.refs_2_.refs_3_.refs_4_.refs_5_.refs_6_.refs_7_ = bf16[8,256,256]{2,1,0:T(8,128)(2,1)S(1)} async-done(((bf16[8,256,256]{2,1,0:T(8,128)(2,1)}), bf16[8,256,256]{2,1,0:T(8,128)(2,1)S(1)}, u32[]{:S(2)}, u32[]{:S(2)}) %all-to-all-start.1) | async-done | bytes 1048608 | tf_op jit(solution)/shard_map/all_to_all | solution.py:529
  326.9 3.0 collective-permute-done.24.refs_5_
  329.9 3.0 shard_map.129
  (151 shorter events, 82.8 us)
Async XLA Ops:
  6.5 101.5 %all-gather.7.cloned.1.call-start = ((), (), s32[]{:S(2)}) async-start(), calls=%async_computation.3 | async-start | bytes 5242880 | tf_op jit(solution)/shard_map/all_gather | solution.py:458
  10.2 166.4 %all-gather.9.cloned.1.call-start = ((), (), s32[]{:S(2)}) async-start(), calls=%async_computation.4 | async-start | bytes 5242880 | tf_op jit(solution)/shard_map/all_gather | solution.py:458
  11.4 238.8 %all-gather.11.cloned.1.call-start = ((), (), s32[]{:S(2)}) async-start(), calls=%async_computation.5 | async-start | bytes 2621440 | tf_op jit(solution)/shard_map/all_gather | solution.py:458
  15.8 4.4 %collective-permute-start.1 = (f32[1024]{0:T(1024)S(1)}, f32[1024]{0:T(1024)S(1)}, u32[]{:S(2)}, u32[]{:S(2)}) collective-permute-start(f32[1024]{0:T(1024)S(1)} %add.48), channel_id=1, source_target_pairs={{0,2},{1,3},{2,0},{3,1},{4,6},{5,7},{6,4},{7,5},{8,10},{9,11},{10,... | collective-permute-start | bytes 12296 | tf_op jit(solution)/shard_map/ppermute | solution.py:444
  25.1 24.5 %collective-permute-start.3 = (bf16[512,1024]{1,0:T(8,128)(2,1)S(1)}, bf16[512,1024]{1,0:T(8,128)(2,1)S(1)}, u32[]{:S(2)}, u32[]{:S(2)}) collective-permute-start(bf16[512,1024]{1,0:T(8,128)(2,1)S(1)} %get-tuple-element.82), channel_id=1, source_target_pairs={{0,2},{1,3},{2,0},{3,1},{4,6},{5,7},{6,4},{7,5},{8,10},{9,11},{10,... | collective-permute-start | bytes 3145736 | tf_op jit(solution)/shard_map/ppermute | solution.py:444
  27.2 24.1 %collective-permute-start.4 = (bf16[512,1024]{1,0:T(8,128)(2,1)S(1)}, bf16[512,1024]{1,0:T(8,128)(2,1)}, u32[]{:S(2)}, u32[]{:S(2)}) collective-permute-start(bf16[512,1024]{1,0:T(8,128)(2,1)S(1)} %get-tuple-element.79), channel_id=1, source_target_pairs={{0,4},{4,0},{8,12},{12,8},{16,20},{20,16},{24,28},{28,24},{1,5},{5... | collective-permute-start | bytes 3145736 | tf_op jit(solution)/shard_map/ppermute | solution.py:441
  51.3 23.3 %collective-permute-start.6 = (bf16[512,1024]{1,0:T(8,128)(2,1)}, bf16[512,1024]{1,0:T(8,128)(2,1)}, u32[]{:S(2)}, u32[]{:S(2)}) collective-permute-start(bf16[512,1024]{1,0:T(8,128)(2,1)} %collective-permute-done.4.refs_0_), channel_id=1, source_target_pairs={{0,2},{1,3},{2,0},{3,1},{4,6},{5,7},{6,4},{7,5},{8,10},{9,11},{10,... | collective-permute-start | bytes 3145736 | tf_op jit(solution)/shard_map/ppermute | solution.py:444
  51.6 23.1 %collective-permute-start.5 = (bf16[512,1024]{1,0:T(8,128)(2,1)S(1)}, bf16[512,1024]{1,0:T(8,128)(2,1)}, u32[]{:S(2)}, u32[]{:S(2)}) collective-permute-start(bf16[512,1024]{1,0:T(8,128)(2,1)S(1)} %get-tuple-element.35), channel_id=1, source_target_pairs={{0,4},{4,0},{8,12},{12,8},{16,20},{20,16},{24,28},{28,24},{1,5},{5... | collective-permute-start | bytes 3145736 | tf_op jit(solution)/shard_map/ppermute | solution.py:441
  74.7 22.4 %collective-permute-start.7 = (bf16[512,1024]{1,0:T(8,128)(2,1)}, bf16[512,1024]{1,0:T(8,128)(2,1)}, u32[]{:S(2)}, u32[]{:S(2)}) collective-permute-start(bf16[512,1024]{1,0:T(8,128)(2,1)} %collective-permute-done.5.refs_0_), channel_id=1, source_target_pairs={{0,2},{1,3},{2,0},{3,1},{4,6},{5,7},{6,4},{7,5},{8,10},{9,11},{10,... | collective-permute-start | bytes 3145736 | tf_op jit(solution)/shard_map/ppermute | solution.py:444
  76.2 22.0 %collective-permute-start.10 = (bf16[512,1024]{1,0:T(8,128)(2,1)}, bf16[512,1024]{1,0:T(8,128)(2,1)}, u32[]{:S(2)}, u32[]{:S(2)}) collective-permute-start(bf16[512,1024]{1,0:T(8,128)(2,1)} %collective-permute-done.4.refs_0_), channel_id=1, source_target_pairs={{0,1},{1,0},{2,3},{3,2},{4,5},{5,4},{6,7},{7,6},{8,9},{9,8},{10,11... | collective-permute-start | bytes 3145736 | tf_op jit(solution)/shard_map/ppermute | solution.py:447
  76.2 22.1 %collective-permute-start.11 = (bf16[512,1024]{1,0:T(8,128)(2,1)}, bf16[512,1024]{1,0:T(8,128)(2,1)}, u32[]{:S(2)}, u32[]{:S(2)}) collective-permute-start(bf16[512,1024]{1,0:T(8,128)(2,1)} %collective-permute-done.6.refs_2_), channel_id=1, source_target_pairs={{0,1},{1,0},{2,3},{3,2},{4,5},{5,4},{6,7},{7,6},{8,9},{9,8},{10,11... | collective-permute-start | bytes 3145736 | tf_op jit(solution)/shard_map/ppermute | solution.py:447
  77.2 26.9 %collective-permute-start.12 = (bf16[512,1024]{1,0:T(8,128)(2,1)}, bf16[512,1024]{1,0:T(8,128)(2,1)S(1)}, u32[]{:S(2)}, u32[]{:S(2)}) collective-permute-start(bf16[512,1024]{1,0:T(8,128)(2,1)} %collective-permute-done.5.refs_0_), channel_id=1, source_target_pairs={{0,1},{1,0},{2,3},{3,2},{4,5},{5,4},{6,7},{7,6},{8,9},{9,8},{10,11... | collective-permute-start | bytes 3145736 | tf_op jit(solution)/shard_map/ppermute | solution.py:447
  97.2 7.0 %collective-permute-start.13 = (bf16[512,1024]{1,0:T(8,128)(2,1)}, bf16[512,1024]{1,0:T(8,128)(2,1)S(1)}, u32[]{:S(2)}, u32[]{:S(2)}) collective-permute-start(bf16[512,1024]{1,0:T(8,128)(2,1)} %collective-permute-done.7.refs_2_), channel_id=1, source_target_pairs={{0,1},{1,0},{2,3},{3,2},{4,5},{5,4},{6,7},{7,6},{8,9},{9,8},{10,11... | collective-permute-start | bytes 3145736 | tf_op jit(solution)/shard_map/ppermute | solution.py:447
  97.6 48.9 %collective-permute-start.2 = (bf16[1024,1024]{1,0:T(8,128)(2,1)S(1)}, bf16[1024,1024]{1,0:T(8,128)(2,1)}, u32[]{:S(2)}, u32[]{:S(2)}) collective-permute-start(bf16[1024,1024]{1,0:T(8,128)(2,1)S(1)} %get-tuple-element.74.refs_0_), channel_id=1, source_target_pairs={{0,1},{1,0},{2,3},{3,2},{4,5},{5,4},{6,7},{7,6},{8,9},{9,8},{10,11... | collective-permute-start | bytes 6291464 | tf_op jit(solution)/shard_map/ppermute | solution.py:447
  98.2 48.3 %collective-permute-start.9 = (bf16[512,1024]{1,0:T(8,128)(2,1)S(1)}, bf16[512,1024]{1,0:T(8,128)(2,1)}, u32[]{:S(2)}, u32[]{:S(2)}) collective-permute-start(bf16[512,1024]{1,0:T(8,128)(2,1)S(1)} %collective-permute-done.3.refs_2_), channel_id=1, source_target_pairs={{0,1},{1,0},{2,3},{3,2},{4,5},{5,4},{6,7},{7,6},{8,9},{9,8},{10,11... | collective-permute-start | bytes 3145736 | tf_op jit(solution)/shard_map/ppermute | solution.py:447
  98.3 25.8 %collective-permute-start.8 = (bf16[512,1024]{1,0:T(8,128)(2,1)}, bf16[512,1024]{1,0:T(8,128)(2,1)}, u32[]{:S(2)}, u32[]{:S(2)}) collective-permute-start(bf16[512,1024]{1,0:T(8,128)(2,1)} %get-tuple-element.38), channel_id=1, source_target_pairs={{0,2},{1,3},{2,0},{3,1},{4,6},{5,7},{6,4},{7,5},{8,10},{9,11},{10,... | collective-permute-start | bytes 3145736 | tf_op jit(solution)/shard_map/ppermute | solution.py:444
  119.8 25.3 %collective-permute-start.15 = (f32[1024,256]{1,0:T(8,128)S(1)}, f32[1024,256]{1,0:T(8,128)S(1)}, u32[]{:S(2)}, u32[]{:S(2)}) collective-permute-start(f32[1024,256]{1,0:T(8,128)S(1)} %get-tuple-element.41), channel_id=1, source_target_pairs={{0,4},{4,0},{8,12},{12,8},{16,20},{20,16},{24,28},{28,24},{1,5},{5... | collective-permute-start | bytes 3145736 | tf_op jit(solution)/shard_map/ppermute | solution.py:441
  124.1 22.4 %collective-permute-start.14 = (bf16[512,1024]{1,0:T(8,128)(2,1)}, bf16[512,1024]{1,0:T(8,128)(2,1)S(1)}, u32[]{:S(2)}, u32[]{:S(2)}) collective-permute-start(bf16[512,1024]{1,0:T(8,128)(2,1)} %collective-permute-done.8.refs_3_), channel_id=1, source_target_pairs={{0,1},{1,0},{2,3},{3,2},{4,5},{5,4},{6,7},{7,6},{8,9},{9,8},{10,11... | collective-permute-start | bytes 3145736 | tf_op jit(solution)/shard_map/ppermute | solution.py:447
  145.0 13.3 %collective-permute-start.16 = (bf16[1024,256]{1,0:T(8,128)(2,1)S(1)}, bf16[1024,256]{1,0:T(8,128)(2,1)S(1)}, u32[]{:S(2)}, u32[]{:S(2)}) collective-permute-start(bf16[1024,256]{1,0:T(8,128)(2,1)S(1)} %get-tuple-element.45), channel_id=1, source_target_pairs={{0,4},{4,0},{8,12},{12,8},{16,20},{20,16},{24,28},{28,24},{1,5},{5... | collective-permute-start | bytes 1572872 | tf_op jit(solution)/shard_map/ppermute | solution.py:441
  170.7 52.4 %all-to-all-start = ((bf16[8,256,256]{2,1,0:T(8,128)(2,1)}), bf16[8,256,256]{2,1,0:T(8,128)(2,1)S(1)}, u32[]{:S(2)}, u32[]{:S(2)}) async-start(bf16[8,256,256]{2,1,0:T(8,128)(2,1)} %shard_map.116), calls=%async_computation | async-start | bytes 2097152 | tf_op jit(solution)/shard_map/all_to_all | solution.py:529
  188.6 15.3 %collective-permute-start.17 = (bf16[1024,256]{1,0:T(8,128)(2,1)S(1)}, bf16[1024,256]{1,0:T(8,128)(2,1)S(1)}, u32[]{:S(2)}, u32[]{:S(2)}) collective-permute-start(bf16[1024,256]{1,0:T(8,128)(2,1)S(1)} %get-tuple-element.48), channel_id=1, source_target_pairs={{0,4},{4,0},{8,12},{12,8},{16,20},{20,16},{24,28},{28,24},{1,5},{5... | collective-permute-start | bytes 1572872 | tf_op jit(solution)/shard_map/ppermute | solution.py:441
  203.9 11.6 %collective-permute-start.18 = (bf16[1024,256]{1,0:T(8,128)(2,1)S(1)}, bf16[1024,256]{1,0:T(8,128)(2,1)S(1)}, u32[]{:S(2)}, u32[]{:S(2)}) collective-permute-start(bf16[1024,256]{1,0:T(8,128)(2,1)S(1)} %get-tuple-element.49), channel_id=1, source_target_pairs={{0,4},{4,0},{8,12},{12,8},{16,20},{20,16},{24,28},{28,24},{1,5},{5... | collective-permute-start | bytes 1572872 | tf_op jit(solution)/shard_map/ppermute | solution.py:441
  223.1 58.8 %all-to-all-start.2 = ((bf16[8,256,256]{2,1,0:T(8,128)(2,1)}), bf16[8,256,256]{2,1,0:T(8,128)(2,1)S(1)}, u32[]{:S(2)}, u32[]{:S(2)}) async-start(bf16[8,256,256]{2,1,0:T(8,128)(2,1)} %shard_map.119), calls=%async_computation.2 | async-start | bytes 2097152 | tf_op jit(solution)/shard_map/all_to_all | solution.py:529
  258.9 14.0 %collective-permute-start.19 = (bf16[1024,256]{1,0:T(8,128)(2,1)S(1)}, bf16[1024,256]{1,0:T(8,128)(2,1)S(1)}, u32[]{:S(2)}, u32[]{:S(2)}) collective-permute-start(bf16[1024,256]{1,0:T(8,128)(2,1)S(1)} %shard_map.122), channel_id=1, source_target_pairs={{0,4},{4,0},{8,12},{12,8},{16,20},{20,16},{24,28},{28,24},{1,5},{5... | collective-permute-start | bytes 1572872 | tf_op jit(solution)/shard_map/ppermute | solution.py:441
  281.9 42.2 %all-to-all-start.1 = ((bf16[8,256,256]{2,1,0:T(8,128)(2,1)}), bf16[8,256,256]{2,1,0:T(8,128)(2,1)S(1)}, u32[]{:S(2)}, u32[]{:S(2)}) async-start(bf16[8,256,256]{2,1,0:T(8,128)(2,1)} %shard_map.121), calls=%async_computation.1 | async-start | bytes 2097152 | tf_op jit(solution)/shard_map/all_to_all | solution.py:529
  295.3 11.7 %collective-permute-start.20 = (bf16[256,256]{1,0:T(8,128)(2,1)S(1)}, bf16[256,256]{1,0:T(8,128)(2,1)S(1)}, u32[]{:S(2)}, u32[]{:S(2)}) collective-permute-start(bf16[256,256]{1,0:T(8,128)(2,1)S(1)} %get-tuple-element.55), channel_id=1, source_target_pairs={{0,4},{4,0},{8,12},{12,8},{16,20},{20,16},{24,28},{28,24},{1,5},{5... | collective-permute-start | bytes 393224 | tf_op jit(solution)/shard_map/ppermute | solution.py:525
  297.3 13.0 %collective-permute-start.21 = (bf16[256,256]{1,0:T(8,128)(2,1)S(1)}, bf16[256,256]{1,0:T(8,128)(2,1)S(1)}, u32[]{:S(2)}, u32[]{:S(2)}) collective-permute-start(bf16[256,256]{1,0:T(8,128)(2,1)S(1)} %get-tuple-element.56), channel_id=1, source_target_pairs={{0,8},{4,12},{8,0},{12,4},{16,24},{20,28},{24,16},{28,20},{1,9},{5... | collective-permute-start | bytes 393224 | tf_op jit(solution)/shard_map/ppermute | solution.py:525
  298.8 27.2 %collective-permute-start.22 = (bf16[256,256]{1,0:T(8,128)(2,1)}, bf16[256,256]{1,0:T(8,128)(2,1)}, u32[]{:S(2)}, u32[]{:S(2)}) collective-permute-start(bf16[256,256]{1,0:T(8,128)(2,1)} %get-tuple-element.57), channel_id=1, source_target_pairs={{0,12},{4,8},{8,4},{12,0},{16,28},{20,24},{24,20},{28,16},{1,13},{... | collective-permute-start | bytes 393224 | tf_op jit(solution)/shard_map/ppermute | solution.py:525
  298.8 28.1 %collective-permute-start.23 = (bf16[256,256]{1,0:T(8,128)(2,1)}, bf16[256,256]{1,0:T(8,128)(2,1)}, u32[]{:S(2)}, u32[]{:S(2)}) collective-permute-start(bf16[256,256]{1,0:T(8,128)(2,1)} %get-tuple-element.58), channel_id=1, source_target_pairs={{0,16},{4,20},{8,24},{12,28},{16,0},{20,4},{24,8},{28,12},{1,17},{... | collective-permute-start | bytes 393224 | tf_op jit(solution)/shard_map/ppermute | solution.py:525
  301.7 28.2 %collective-permute-start.24 = (bf16[256,256]{1,0:T(8,128)(2,1)}, bf16[256,256]{1,0:T(8,128)(2,1)}, u32[]{:S(2)}, u32[]{:S(2)}) collective-permute-start(bf16[256,256]{1,0:T(8,128)(2,1)} %get-tuple-element.59), channel_id=1, source_target_pairs={{0,20},{4,16},{8,28},{12,24},{16,4},{20,0},{24,12},{28,8},{1,21},{... | collective-permute-start | bytes 393224 | tf_op jit(solution)/shard_map/ppermute | solution.py:525
  307.0 22.9 %collective-permute-start.25 = (bf16[256,256]{1,0:T(8,128)(2,1)}, bf16[256,256]{1,0:T(8,128)(2,1)S(1)}, u32[]{:S(2)}, u32[]{:S(2)}) collective-permute-start(bf16[256,256]{1,0:T(8,128)(2,1)} %get-tuple-element.60), channel_id=1, source_target_pairs={{0,24},{4,28},{8,16},{12,20},{16,8},{20,12},{24,0},{28,4},{1,25},{... | collective-permute-start | bytes 393224 | tf_op jit(solution)/shard_map/ppermute | solution.py:525
  311.0 19.0 %collective-permute-start.26 = (bf16[256,256]{1,0:T(8,128)(2,1)S(1)}, bf16[256,256]{1,0:T(8,128)(2,1)S(1)}, u32[]{:S(2)}, u32[]{:S(2)}) collective-permute-start(bf16[256,256]{1,0:T(8,128)(2,1)S(1)} %get-tuple-element.61), channel_id=1, source_target_pairs={{0,28},{4,24},{8,20},{12,16},{16,12},{20,8},{24,4},{28,0},{1,29},{... | collective-permute-start | bytes 393224 | tf_op jit(solution)/shard_map/ppermute | solution.py:525
  (34 other events, 481.9 us)
Sparse Core Ops, SparseCore 0:
  10.4 83.4 all-gather.6
  95.4 79.2 all-gather.8
  176.3 73.7 all-gather.10
